TPU v7x, 512 devices: a whole 4x8x8 slice. The times are simulated.
512 devices in a mesh: section: 32 (over z, x), leaf: 16 (over y, core).
Axes of the slice: x: 4, y: 8, z: 8, core: 2. Of those that a mesh axis runs over, the one named last changes fastest.
Arguments:
- query_feats: bfloat16 [65536, 300], P(('section', 'leaf')), may hold values from -6 to 6
- query_weight: float32 [65536], P('section'), may hold values from 0.02 to 0.2
- positive_label: int32 [65536, 8], P('section'), may hold values from 0 to 131071, as said below
- positive_bucket: int32 [65536, 8], P('section'), may hold values from 0 to 15
- inv_prop: float32 [16], replicated, may hold values from 1 to 10
- primary_w: bfloat16 [131072, 300], P(('section', 'leaf')), may hold values from -0.375 to 0.375
- copy_owner: int32 [131072], P(('section', 'leaf')), may hold values from 0 to 31, as said below
- copy_row: int32 [131072], P(('section', 'leaf')), may hold values from 0 to 255
Outputs:
- query_grad: float32 [65536, 300], P(('section', 'leaf'))
- primary_grad: float32 [131072, 300], P(('section', 'leaf'))
Inputs may be any that keep to these rules, and one draw needn't show every extreme that they name: `copy_owner`: each copy names a section other than its own device's; among the copies of one device at most 16 name one owner, and exactly 16 name one of them. `positive_label`: every listed label is the label of some slot, primary or copy, of the query's own section; a label may be listed twice.
All inputs are finite; a program needn't handle non-finite values.
Results may differ from a plain program's by a relative error of at most 0.0018.
Values may be sent and summed in bfloat16 or wider, within the bound.
No kernel may reach another device: no remote copies, remote signals or barrier semaphores. Data moves between devices by JAX's collectives and lax.ppermute only.
A program may use at most 64 MiB of HBM per device.

v0:
```python
import math

import jax
import jax.numpy as jnp
from jax import lax
from jax.sharding import PartitionSpec as P


def on_device(
    query_feats,
    query_weight,
    positive_label,
    positive_bucket,
    inv_prop,
    primary_w,
    copy_owner,
    copy_row,
):
    sections = lax.axis_size("section")
    leaves = lax.axis_size("leaf")
    section_id = lax.axis_index("section")
    leaf_id = lax.axis_index("leaf")
    prim_rows = primary_w.shape[0]
    copy_count = copy_owner.shape[0]
    feature_dim = primary_w.shape[1]
    capacity = 8 * ((2 * copy_count // (sections - 1) + 7) // 8)
    owner_hot = (copy_owner[:, None] == jnp.arange(sections, dtype=jnp.int32)[None, :]).astype(
        jnp.float32
    )
    before = jnp.cumsum(owner_hot, axis=0) - owner_hot
    rank_in = jnp.sum(before * owner_hot, axis=1).astype(jnp.int32)
    target = copy_owner * capacity + rank_in
    requests = (
        jnp.zeros((sections * capacity,), jnp.int32)
        .at[target]
        .set(copy_row)
        .reshape(sections, capacity)
    )
    wanted = lax.all_to_all(requests, "section", split_axis=0, concat_axis=0, tiled=True)
    served = jnp.take(primary_w, wanted.reshape(-1), axis=0).reshape(
        sections, capacity, feature_dim
    )
    arrived = lax.all_to_all(served, "section", split_axis=0, concat_axis=0, tiled=True)
    copy_w = jnp.take(arrived.reshape(sections * capacity, feature_dim), target, axis=0)
    weights = jnp.concatenate([primary_w, copy_w], axis=0)
    first_label = (section_id * leaves + leaf_id) * prim_rows
    labels = jnp.concatenate(
        [
            first_label + jnp.arange(prim_rows, dtype=jnp.int32),
            (copy_owner * leaves + leaf_id) * prim_rows + copy_row,
        ]
    )
    bucket_hot = positive_bucket[..., None] == jnp.arange(inv_prop.shape[0], dtype=jnp.int32)
    pos_value = jnp.sum(jnp.where(bucket_hot, inv_prop, 0.0), axis=-1)
    slot_count = weights.shape[0]
    section_rows = positive_label.shape[0]
    start_state = (
        jnp.zeros((slot_count, feature_dim), jnp.float32),
        jnp.zeros((section_rows, feature_dim), jnp.float32),
    )
    shard_rows = lax.all_gather(query_feats, "leaf", axis=0, tiled=True)
    piece_rows = shard_rows.shape[0]
    block_rows = math.gcd(piece_rows, 256)

    def block_step(block_num, partial_sums):
        slot_acc, query_acc = partial_sums
        offset_row = block_num * block_rows
        q_block = lax.dynamic_slice_in_dim(shard_rows, offset_row, block_rows, 0)
        labels_block = lax.dynamic_slice_in_dim(positive_label, offset_row, block_rows, 0)
        values_block = lax.dynamic_slice_in_dim(pos_value, offset_row, block_rows, 0)
        scale_block = lax.dynamic_slice_in_dim(query_weight, offset_row, block_rows, 0)
        logits = lax.dot_general(
            q_block, weights, (((1,), (1,)), ((), ())), preferred_element_type=jnp.float32
        )
        sigmoid_val = jax.nn.sigmoid(logits)
        hit_count = jnp.zeros(logits.shape, jnp.float32)
        pos_weight = jnp.zeros(logits.shape, jnp.float32)
        for column in range(labels_block.shape[1]):
            matched = (labels[None, :] == labels_block[:, column : column + 1]).astype(jnp.float32)
            hit_count = hit_count + matched
            pos_weight = pos_weight + matched * values_block[:, column : column + 1]
        mixed = (1.0 - jnp.minimum(hit_count, 1.0)) * sigmoid_val + pos_weight * (sigmoid_val - 1.0)
        coefficient = (scale_block[:, None] * mixed).astype(jnp.bfloat16)
        query_part = jnp.dot(coefficient, weights, preferred_element_type=jnp.float32)
        query_acc = lax.dynamic_update_slice_in_dim(query_acc, query_part, offset_row, 0)
        slot_acc = slot_acc + lax.dot_general(
            coefficient, q_block, (((0,), (0,)), ((), ())), preferred_element_type=jnp.float32
        )
        return (slot_acc, query_acc)

    slot_grad, query_sum = lax.fori_loop(0, piece_rows // block_rows, block_step, start_state)
    send_back = (
        jnp.zeros((sections * capacity, feature_dim), jnp.float32)
        .at[target]
        .set(slot_grad[prim_rows:])
        .reshape(sections, capacity, feature_dim)
    )
    returned = lax.all_to_all(send_back, "section", split_axis=0, concat_axis=0, tiled=True)
    primary_grad = (
        slot_grad[:prim_rows].at[wanted.reshape(-1)].add(returned.reshape(-1, feature_dim))
    )
    query_whole = lax.psum(query_sum, "leaf")
    query_grad = lax.dynamic_slice_in_dim(
        query_whole, leaf_id * query_feats.shape[0], query_feats.shape[0], 0
    )
    return (query_grad, primary_grad)


def solution(mesh):
    placed = (
        P(("section", "leaf"), None),
        P("section"),
        P("section", None),
        P("section", None),
        P(),
        P(("section", "leaf"), None),
        P(("section", "leaf")),
        P(("section", "leaf")),
    )
    return jax.shard_map(
        on_device,
        mesh=mesh,
        in_specs=placed,
        out_specs=(P(("section", "leaf"), None), P(("section", "leaf"), None)),
        check_vma=False,
    )
```

profile of v0, /device:TPU:1, one launch (start us, length us, event | category | flops | bytes accessed | tf_op | source)
XLA Modules:
  0.0 240.9 jit_solution(1173304423045071907)
XLA Ops:
  7.2 1.6 copy.31
  11.8 1.6 scatter_custom_fusion
  14.0 13.7 %all-to-all-start = ((s32[32,1,16]{2,1,0:T(1,128)}), s32[32,1,16]{2,1,0:T(1,128)S(1)}, u32[]{:S(2)}, u32[]{:S(2)}) async-start(s32[32,1,16]{2,1,0:T(1,128)} %bitcast.2), calls=%async_computation | async-start | bytes 32768 | tf_op jit(solution)/shard_map/all_to_all | solution.py:39
  28.9 7.4 %all-to-all-done = s32[32,1,16]{2,1,0:T(1,128)S(1)} async-done(((s32[32,1,16]{2,1,0:T(1,128)}), s32[32,1,16]{2,1,0:T(1,128)S(1)}, u32[]{:S(2)}, u32[]{:S(2)}) %all-to-all-start) | async-done | bytes 2080 | tf_op jit(solution)/shard_map/all_to_all | solution.py:39
  37.6 1.9 gather_fusion
  40.5 3.9 %all-to-all-start.1 = ((bf16[32,16,300]{2,1,0:T(8,128)(2,1)}), bf16[32,16,300]{2,1,0:T(8,128)(2,1)S(1)}, u32[]{:S(2)}, u32[]{:S(2)}) async-start(bf16[32,16,300]{2,1,0:T(8,128)(2,1)} %broadcast_select_fusion), calls=%async_computation.1 | async-start | bytes 786432 | tf_op jit(solution)/shard_map/all_to_all | solution.py:43
  45.4 10.8 %all-to-all-done.1 = bf16[32,16,300]{2,1,0:T(8,128)(2,1)S(1)} async-done(((bf16[32,16,300]{2,1,0:T(8,128)(2,1)}), bf16[32,16,300]{2,1,0:T(8,128)(2,1)S(1)}, u32[]{:S(2)}, u32[]{:S(2)}) %all-to-all-start.1) | async-done | bytes 307232 | tf_op jit(solution)/shard_map/all_to_all | solution.py:43
  58.3 51.9 %while.18 = (s32[]{:T(128)}, f32[512,300]{0,1:T(8,128)S(1)}, f32[2048,300]{0,1:T(8,128)S(1)}, f32[2048]{0:T(1024)}, s32[512]{0:T(512)S(1)}, /*index=5*/s32[2048,...) while((s32[]{:T(128)}, f32[512,300]{0,1:T(8,128)S(1)}, ...), condition=%wide.region_6.7_spmd.clone, body=%wide.region_5.6_spmd.clone.sunk | while | flops 242659344 | bytes 3474841 | solution.py:91
  61.3 2.0 fusion.53
  63.2 1.2 convolution_add_fusion.2
  67.8 2.0 fusion.53
  74.2 2.0 fusion.53
  80.7 2.0 fusion.53
  87.2 2.0 fusion.53
  93.7 2.0 fusion.53
  100.2 2.0 fusion.53
  106.7 2.0 fusion.53
  110.2 1.4 copy-done
  111.9 2.3 scatter_custom_fusion.1
  114.2 10.0 %all-to-all-start.2 = ((f32[32,16,300]{2,1,0:T(8,128)}), f32[32,16,300]{2,1,0:T(8,128)S(1)}, u32[]{:S(2)}, u32[]{:S(2)}) async-start(f32[32,16,300]{2,1,0:T(8,128)} %bitcast.7), calls=%async_computation.2 | async-start | bytes 1572864 | tf_op jit(solution)/shard_map/all_to_all | solution.py:98
  124.5 21.2 %all-to-all-done.2 = f32[32,16,300]{2,1,0:T(8,128)S(1)} async-done(((f32[32,16,300]{2,1,0:T(8,128)}), f32[32,16,300]{2,1,0:T(8,128)S(1)}, u32[]{:S(2)}, u32[]{:S(2)}) %all-to-all-start.2) | async-done | bytes 614432 | tf_op jit(solution)/shard_map/all_to_all | solution.py:98
  145.7 3.8 %scatter_fusion = f32[256,300]{1,0:T(8,128)S(1)} fusion(f32[256,300]{1,0:T(8,128)S(1)} %slice.197, s32[512]{0:T(512)S(1)} %bitcast.110, f32[512,300]{1,0:T(8,128)S(1)} %bitcast.90), kind=kCustom, calls=%fused_computation.4 | custom fusion | flops 153600 | bytes 1845248 | tf_op jit(solution)/shard_map/scatter-add | solution.py:100
  150.3 82.2 %all-reduce.2.cloned.1.call-done = f32[2048,300]{0,1:T(8,128)} async-done(((f32[2048,300]{0,1:T(8,128)}), f32[2048,300]{0,1:T(8,128)}) %all-reduce.2.cloned.1.call-update) | async-done | bytes 2457616 | tf_op jit(solution)/shard_map/psum | solution.py:102
  232.5 1.6 constant_dynamic-slice_fusion.2
  (84 shorter events, 45.8 us)
Async XLA Ops:
  7.2 50.9 %all-gather.2.cloned.1.call-start = ((), (), s32[]{:S(2)}) async-start(), calls=%async_computation.3 | async-start | bytes 1671168 | tf_op jit(solution)/shard_map/all_gather | solution.py:61
  14.0 22.2 %all-to-all-start = ((s32[32,1,16]{2,1,0:T(1,128)}), s32[32,1,16]{2,1,0:T(1,128)S(1)}, u32[]{:S(2)}, u32[]{:S(2)}) async-start(s32[32,1,16]{2,1,0:T(1,128)} %bitcast.2), calls=%async_computation | async-start | bytes 32768 | tf_op jit(solution)/shard_map/all_to_all | solution.py:39
  37.6 6.9 %copy-start.2 = (s32[256]{0:T(256)S(1)}, s32[256]{0:T(256)}, u32[]{:S(2)}) copy-start(s32[256]{0:T(256)} %param.16) | copy-start | bytes 3076
  37.6 6.9 %copy-start.3 = (s32[256]{0:T(256)S(1)}, s32[256]{0:T(256)}, u32[]{:S(2)}) copy-start(s32[256]{0:T(256)} %param.17) | copy-start | bytes 3076
  37.6 6.9 %copy-start.1 = (s32[2048,8]{0,1:T(8,128)S(1)}, s32[2048,8]{0,1:T(8,128)}, u32[]{:S(2)}) copy-start(s32[2048,8]{0,1:T(8,128)} %param.13) | copy-start | bytes 196612
  37.6 6.9 %copy-start.4 = (f32[16]{0:T(128)S(1)}, f32[16]{0:T(128)}, u32[]{:S(2)}) copy-start(f32[16]{0:T(128)} %param.14) | copy-start | bytes 196
  40.5 15.8 %all-to-all-start.1 = ((bf16[32,16,300]{2,1,0:T(8,128)(2,1)}), bf16[32,16,300]{2,1,0:T(8,128)(2,1)S(1)}, u32[]{:S(2)}, u32[]{:S(2)}) async-start(bf16[32,16,300]{2,1,0:T(8,128)(2,1)} %broadcast_select_fusion), calls=%async_computation.1 | async-start | bytes 786432 | tf_op jit(solution)/shard_map/all_to_all | solution.py:43
  44.4 188.1 %all-reduce.2.cloned.1.call-start = ((), (), s32[]{:S(2)}) async-start(), calls=%async_computation.4 | async-start | bytes 4980736 | tf_op jit(solution)/shard_map/psum | solution.py:102
  110.2 1.5 copy-start
  114.2 31.5 %all-to-all-start.2 = ((f32[32,16,300]{2,1,0:T(8,128)}), f32[32,16,300]{2,1,0:T(8,128)S(1)}, u32[]{:S(2)}, u32[]{:S(2)}) async-start(f32[32,16,300]{2,1,0:T(8,128)} %bitcast.7), calls=%async_computation.2 | async-start | bytes 1572864 | tf_op jit(solution)/shard_map/all_to_all | solution.py:98
Sparse Core Ops, SparseCore 0:
  10.7 47.2 all-gather.1
  111.8 120.6 all-reduce.1
where the time goes:
time: 243 us; the launch traced here: 241 us
  waiting for transfers between devices  122 us (50%)
  local copies, waits for them, and re-layouts  39.2 us (16%)
  matrix products  28 us (12%)
  starting transfers between devices  27.7 us (11%)
  between operations  14.3 us (6%)
  other arithmetic  9.21 us (4%)
    psum x1, waiting for transfers between devices, on_device(): query_whole = lax.psum(query_sum, 'leaf')  82.2 us
    all_to_all x1, waiting for transfers between devices, on_device(): lax.all_to_all(send_back, 'section', split_axis=0, concat_axis=0, tiled=T...  21.2 us
    dot_general x8, matrix products, block_step(): lax.dot_general(q_block, weights, (((1,), (1,)), ((), ())), preferred_ele...  15.7 us
    all_to_all x1, starting transfers between devices, on_device(): lax.all_to_all(requests, 'section', split_axis=0, concat_axis=0, tiled=True)  13.7 us
    all_to_all x1, waiting for transfers between devices, on_device(): lax.all_to_all(served, 'section', split_axis=0, concat_axis=0, tiled=True)  10.8 us
    all_to_all x1, starting transfers between devices, on_device(): lax.all_to_all(send_back, 'section', split_axis=0, concat_axis=0, tiled=T...  10 us
    dot_general x8, matrix products, block_step(): lax.dot_general(coefficient, q_block, (((0,), (0,)), ((), ())), preferred...  10 us
    slice x8, local copies, waits for them, and re-layouts, block_step(): labels_block[:, column:column + 1]  8.72 us
  transfers between devices with their start and end apart: 5, of which 5 were waited for; matrix products, arithmetic and copies ran while one was open for 8% of the time, Pallas kernels for 0%

commit v1 on v0

v1 whole, which is shorter than its diff:
```python
import functools

import jax
import jax.numpy as jnp
from jax import lax
from jax.experimental import pallas as pl
from jax.experimental.pallas import tpu as pltpu
from jax.sharding import PartitionSpec as P

BF16 = jnp.bfloat16
F32 = jnp.float32
I32 = jnp.int32
LANES = 128
CAP = 16
ROW_CHUNK = 32

VMEM = pl.BlockSpec(memory_space=pltpu.VMEM)
SMEM = pl.BlockSpec(memory_space=pltpu.SMEM)
PARAMS = pltpu.CompilerParams(vmem_limit_bytes=40 * 2**20)


def iota(shape, dim):
    return lax.broadcasted_iota(I32, shape, dim)


def ones(mask):
    return jnp.where(mask, 1.0, 0.0).astype(BF16)


def nt(a, b):
    return lax.dot_general(a, b, (((1,), (1,)), ((), ())), preferred_element_type=F32)


def nn(a, b):
    return lax.dot_general(a, b, (((1,), (0,)), ((), ())), preferred_element_type=F32)


def tn(a, b):
    return lax.dot_general(a, b, (((0,), (0,)), ((), ())), preferred_element_type=F32)


def call(kernel, out, ins, scratch=(), flops=0, size=0):
    return pl.pallas_call(
        kernel,
        out_shape=out,
        in_specs=ins,
        out_specs=jax.tree.map(lambda _: VMEM, out),
        scratch_shapes=scratch,
        compiler_params=PARAMS,
        cost_estimate=pl.CostEstimate(flops=flops, bytes_accessed=size, transcendentals=0),
    )


def ranks(owner, sections):
    n = owner.shape[1]
    hot = owner == iota((sections, n), 0)
    upper = ones(iota((n, n), 0) < iota((n, n), 1))
    before = nn(ones(hot), upper)
    return hot, jnp.sum(jnp.where(hot, before, 0.0), axis=0, keepdims=True)


def ask_kernel(owner_ref, row_ref, ask_ref):
    sections = ask_ref.shape[0]
    owner = owner_ref[...]
    hot, rank = ranks(owner, sections)
    rows = jnp.where(hot, row_ref[...].astype(F32) + 1.0, 0.0).astype(BF16)
    place = ones(iota((LANES, owner.shape[1]), 0).astype(F32) == rank)
    ask_ref[...] = nt(rows, place).reshape(ask_ref.shape)


def wanted_hot(ask, prim):
    sections = ask.shape[0]
    places = sections * CAP
    spread = ones(iota((places, sections), 0) // CAP == iota((places, sections), 1))
    every = nn(spread, ask.astype(BF16))
    mine = iota((places, LANES), 0) % CAP == iota((places, LANES), 1)
    column = jnp.sum(jnp.where(mine, every, 0.0), axis=1, keepdims=True)
    return ones(iota((places, prim), 1).astype(F32) + 1.0 == column)


def serve_kernel(ask_ref, wt_ref, served_ref):
    ask = ask_ref[...].reshape(ask_ref.shape[0], LANES)
    hot = wanted_hot(ask, wt_ref.shape[1])
    served_ref[...] = nt(hot, wt_ref[...]).astype(BF16).reshape(served_ref.shape)


def prepare_kernel(
    first_ref, prop_ref, owner_ref, row_ref, wt_ref, bucket_ref, weight_ref,
    comp_ref, comp_t_ref, slots_ref, wrow_ref, value_ref,
):
    sections = comp_ref.shape[1] // CAP
    owner = owner_ref[...]
    prim = wt_ref.shape[1]
    n = owner.shape[1]
    _, rank = ranks(owner, sections)
    target = owner.astype(F32) * CAP + rank
    places = sections * CAP
    comp_t_ref[...] = ones(iota((places, n), 0).astype(F32) == target)
    target_col = jnp.broadcast_to(target, (LANES, n)).T
    for block in range(places // LANES):
        comp_ref[:, block * LANES:(block + 1) * LANES] = ones(
            (iota((n, LANES), 1) + block * LANES).astype(F32) == target_col
        )
    first = first_ref[0]
    leaf_base = first_ref[1]
    stride = first_ref[2]
    slots_ref[:prim, :] = iota((prim, LANES), 0) + first
    label = owner * stride + leaf_base + row_ref[...]
    slots_ref[prim:, :] = jnp.broadcast_to(label, (LANES, n)).T
    wrow_ref[...] = (wt_ref[...].astype(F32).T * 0.5).astype(BF16)
    bucket = bucket_ref[...]
    value = jnp.zeros(bucket.shape, F32)
    for b in range(prop_ref.shape[0]):
        value = jnp.where(bucket == b, prop_ref[b], value)
    value_ref[...] = value * weight_ref[...] * 0.5


def grad_kernel(
    core_ref, comp_ref, comp_t_ref, slots_ref, wrow_ref, wt_ref, arrived_ref, label_ref, value_ref, weight_ref,
    sib_ref, own_ref,
    part_sib_ref, part_own_ref, prim_ref, back_ref,
    w_scr, wt_scr, logit_scr, coef_scr, copy_scr,
):
    prim = wt_ref.shape[1]
    slots = slots_ref.shape[0]
    dim = wt_ref.shape[0]
    arrived = arrived_ref[...].reshape(-1, dim)
    copies = nn(comp_ref[...], arrived)
    w_scr[:prim, :] = wrow_ref[...]
    w_scr[prim:, :] = (copies * 0.5).astype(BF16)
    wt_scr[:, :prim] = wt_ref[...]
    wt_scr[:, prim:] = copies.T.astype(BF16)
    prim_ref[...] = jnp.zeros(prim_ref.shape, F32)
    copy_scr[...] = jnp.zeros(copy_scr.shape, F32)
    core = core_ref[0]

    def half(q_ref, part_ref, which):
        def step(k, carry):
            q = jnp.concatenate([q_ref[2 * k], q_ref[2 * k + 1]], axis=1)
            logit_scr[...] = nn(w_scr[...], q)
            for side in range(2):
                block = 2 * (2 * k + side) + which
                at = pl.ds(pl.multiple_of(block * LANES, LANES), LANES)
                half_weight = weight_ref[:, at] * 0.5
                labels = label_ref[:, at]
                values = value_ref[:, at]
                lanes = slice(side * LANES, (side + 1) * LANES)
                for r in range(0, slots, ROW_CHUNK):
                    rows = slice(r, r + ROW_CHUNK)
                    t = jnp.tanh(logit_scr[rows, lanes])
                    slot = slots_ref[rows, :]
                    total = jnp.where(slot == labels[0:1, :], values[0:1, :], 0.0)
                    for p in range(1, labels.shape[0]):
                        total = total + jnp.where(slot == labels[p:p + 1, :], values[p:p + 1, :], 0.0)
                    hit = total > 0.0
                    scale = jnp.where(hit, total, half_weight)
                    coef_scr[rows, lanes] = (scale * (t + jnp.where(hit, -1.0, 1.0))).astype(BF16)
            coef = coef_scr[...]
            part = nn(wt_scr[...], coef)
            part_ref[2 * k] = part[:, :LANES]
            part_ref[2 * k + 1] = part[:, LANES:]
            prim_ref[...] += nt(q, coef[:prim])
            copy_scr[...] += nt(coef[prim:], q)
            return carry

        lax.fori_loop(0, q_ref.shape[0] // 2, step, 0)

    half(sib_ref, part_sib_ref, 1 - core)
    half(own_ref, part_own_ref, core)
    back = nn(comp_t_ref[...], copy_scr[...].astype(BF16))
    back_ref[...] = back.astype(BF16).reshape(back_ref.shape)


def finish_kernel(ask_ref, prim_ref, returned_ref, out_ref):
    ask = ask_ref[...].reshape(ask_ref.shape[0], LANES)
    hot = wanted_hot(ask, prim_ref.shape[1])
    returned = returned_ref[...].reshape(-1, prim_ref.shape[0])
    out_ref[...] = prim_ref[...] + tn(returned, hot)


def on_device(
    query_feats, query_weight, positive_label, positive_bucket, inv_prop, primary_w, copy_owner, copy_row
):
    sections = lax.axis_size("section")
    leaves = lax.axis_size("leaf")
    section_id = lax.axis_index("section")
    leaf_id = lax.axis_index("leaf")
    prim, dim = primary_w.shape
    n = copy_owner.shape[0]
    slots = prim + n
    chips = leaves // 2
    same_core = [[2 * y + c for y in range(chips)] for c in range(2)]
    sibling = [(i, i ^ 1) for i in range(leaves)]
    queries = query_feats.shape[0]
    shape = jax.ShapeDtypeStruct

    owner = copy_owner.reshape(1, n)
    row = copy_row.reshape(1, n)
    wt = primary_w.T
    qt = query_feats.T

    ask = call(ask_kernel, shape((sections, 1, LANES), F32), [VMEM] * 2)(owner, row)
    wanted = lax.all_to_all(ask, "section", split_axis=0, concat_axis=0, tiled=True)
    q_own = lax.all_gather(qt, "leaf", axis=0, tiled=False, axis_index_groups=same_core)
    q_sib = lax.ppermute(q_own, "leaf", sibling)
    served = call(serve_kernel, shape((sections, CAP, dim), BF16), [VMEM] * 2)(wanted, wt)
    arrived = lax.all_to_all(served, "section", split_axis=0, concat_axis=0, tiled=True)

    first = (section_id * leaves + leaf_id) * prim
    numbers = jnp.stack([first, leaf_id * prim, jnp.int32(leaves * prim)]).astype(I32)
    weight = query_weight.reshape(1, -1)
    comp, comp_t, slot_ids, wrow, value = call(
        prepare_kernel,
        (
            shape((n, sections * CAP), BF16),
            shape((sections * CAP, n), BF16),
            shape((slots, LANES), I32),
            shape((prim, dim), BF16),
            shape(positive_label.shape[::-1], F32),
        ),
        [SMEM, SMEM] + [VMEM] * 5,
    )(numbers, inv_prop, owner, row, wt, positive_bucket.T, weight)

    core = (leaf_id % 2).reshape(1).astype(I32)
    part_sib, part_own, prim_t, back = call(
        grad_kernel,
        (
            shape((chips, dim, queries), F32),
            shape((chips, dim, queries), F32),
            shape((dim, prim), F32),
            shape((sections, CAP, dim), BF16),
        ),
        [SMEM] + [VMEM] * 11,
        scratch=(
            pltpu.VMEM((slots, dim), BF16),
            pltpu.VMEM((dim, slots), BF16),
            pltpu.VMEM((slots, 2 * LANES), F32),
            pltpu.VMEM((slots, 2 * LANES), BF16),
            pltpu.VMEM((n, dim), F32),
        ),
    )(core, comp, comp_t, slot_ids, wrow, wt, arrived, positive_label.T, value, weight, q_sib, q_own)

    other = lax.ppermute(part_sib, "leaf", sibling)
    returned = lax.all_to_all(back, "section", split_axis=0, concat_axis=0, tiled=True)
    pair = (part_own + other).astype(BF16)
    pieces = lax.all_to_all(pair, "leaf", split_axis=0, concat_axis=0, axis_index_groups=same_core, tiled=True)
    query_grad = jnp.sum(pieces.astype(F32), axis=0)
    prim_grad = call(finish_kernel, shape((dim, prim), F32), [VMEM] * 3)(wanted, prim_t, returned)
    return query_grad.T, prim_grad.T


def solution(mesh):
    placed = (
        P(("section", "leaf"), None),
        P("section"),
        P("section", None),
        P("section", None),
        P(),
        P(("section", "leaf"), None),
        P(("section", "leaf")),
        P(("section", "leaf")),
    )
    return jax.shard_map(
        on_device,
        mesh=mesh,
        in_specs=placed,
        out_specs=(P(("section", "leaf"), None), P(("section", "leaf"), None)),
        check_vma=False,
    )
```

time: 243 us -> 137 us (0.56)
  waiting for transfers between devices: 122 us -> 40.5 us
  local copies, waits for them, and re-layouts: 39.2 us -> 10.3 us
  matrix products: 28 us -> 0 us
  blocking collectives: 0 us -> 22 us
  starting transfers between devices: 27.7 us -> 44.6 us
  Pallas kernels: 0 us -> 15 us
  between operations: 14.3 us -> 0.83 us
  other arithmetic: 9.21 us -> 1.93 us
    psum x1 -> x0, waiting for transfers between devices: 82.2 us -> none  [on_device(): query_whole = lax.psum(query_sum, 'leaf')]
    dot_general x24 -> x0, matrix products: 28 us -> none  [the longest x8 15.7 us: block_step(): lax.dot_general(q_block, weights, (((1,), (1,)), ((), ())), preferred_ele...]
    all_gather x0 -> x1, blocking collectives: none -> 22 us  [on_device(): lax.all_gather(qt, 'leaf', axis=0, tiled=False, axis_index_groups=same_core)]
    slice x19 -> x0, local copies, waits for them, and re-layouts: 17.5 us -> none  [the longest x8 8.72 us: block_step(): labels_block[:, column:column + 1]]
    pallas_call x0 -> x5, Pallas kernels: none -> 15 us  [the longest x1 10.7 us: on_device(): call(grad_kernel, (shape((chips, dim, queries), F32), shape((chips, dim,...]
    ppermute x0 -> x2, starting transfers between devices: none -> 12 us  [the longest x1 8.29 us: on_device(): q_sib = lax.ppermute(q_own, 'leaf', sibling)]
    dynamic_slice x9 -> x0, local copies, waits for them, and re-layouts: 7.7 us -> none  [the longest x8 6.11 us: block_step(): lax.dynamic_slice_in_dim(query_weight, offset_row, block_rows, 0)]
    all_to_all x1, starting transfers between devices: 3.88 us -> 9.7 us  [on_device(): lax.all_to_all(served, 'section', split_axis=0, concat_axis=0, tiled=True)]
  transfers between devices with their start and end apart: 5 -> 6, of which waited for: 5 -> 3; matrix products, arithmetic and copies ran while one was open for 8% -> 1% of each run, Pallas kernels for 0% -> 3%
where the time goes in v1:
time: 137 us; the launch traced here: 135 us
  starting transfers between devices  44.6 us (33%)
  waiting for transfers between devices  40.5 us (30%)
  blocking collectives  22 us (16%)
  Pallas kernels  15 us (11%)
  local copies, waits for them, and re-layouts  10.3 us (8%)
  other arithmetic  1.93 us (1%)
    all_gather x1, blocking collectives, on_device(): lax.all_gather(qt, 'leaf', axis=0, tiled=False, axis_index_groups=same_core)  22 us
    all_to_all x1, waiting for transfers between devices, on_device(): lax.all_to_all(pair, 'leaf', split_axis=0, concat_axis=0, axis_index_grou...  16.6 us
    all_to_all x1, starting transfers between devices, on_device(): lax.all_to_all(ask, 'section', split_axis=0, concat_axis=0, tiled=True)  13.7 us
    all_to_all x1, waiting for transfers between devices, on_device(): lax.all_to_all(back, 'section', split_axis=0, concat_axis=0, tiled=True)  13.3 us
    pallas_call x1, Pallas kernels, on_device(): call(grad_kernel, (shape((chips, dim, queries), F32), shape((chips, dim,...  10.7 us
    all_to_all x1, waiting for transfers between devices, on_device(): lax.all_to_all(served, 'section', split_axis=0, concat_axis=0, tiled=True)  10.6 us
    all_to_all x1, starting transfers between devices, on_device(): lax.all_to_all(served, 'section', split_axis=0, concat_axis=0, tiled=True)  9.7 us
    unnamed x38, local copies, waits for them, and re-layouts  8.68 us
  transfers between devices with their start and end apart: 6, of which 3 were waited for; matrix products, arithmetic and copies ran while one was open for 1% of the time, Pallas kernels for 3%

profile of v1, /device:TPU:1, one launch (start us, length us, event | category | flops | bytes accessed | tf_op | source)
XLA Modules:
  0.0 135.3 jit_solution(4146149903037630833)
XLA Ops:
  0.7 0.7 copy-done.14
  2.0 0.9 shard_map.96
  3.0 13.7 %all-to-all-start = ((f32[32,1,128]{2,1,0:T(1,128)}), f32[32,1,128]{2,1,0:T(1,128)S(1)}, u32[]{:S(2)}, u32[]{:S(2)}) async-start(f32[32,1,128]{2,1,0:T(1,128)} %shard_map.96), calls=%async_computation | async-start | bytes 32768 | tf_op jit(solution)/shard_map/all_to_all | solution.py:203
  16.7 22.0 %all-gather.1.own_ref = bf16[8,300,128]{2,1,0:T(8,128)(2,1)S(1)} all-gather(bf16[1,300,128]{2,1,0:T(8,128)(2,1)} %bitcast.27), channel_id=2, replica_groups={{0,2,4,6,8,10,12,14},{1,3,5,7,9,11,13,15},{16,18,20,22,24,26,28,30},{17..., dimensions={0}, use_global_device_ids=true | all-gather | bytes 691200 | tf_op jit(solution)/shard_map/all_gather | solution.py:204
  38.9 8.3 %collective-permute-start = (bf16[8,300,128]{2,0,1:T(8,128)(2,1)S(1)}, bf16[8,300,128]{2,0,1:T(8,128)(2,1)S(1)}, u32[]{:S(2)}, u32[]{:S(2)}) collective-permute-start(bf16[8,300,128]{2,0,1:T(8,128)(2,1)S(1)} %copy.10), channel_id=1, source_target_pairs={{0,1},{1,0},{2,3},{3,2},{4,5},{5,4},{6,7},{7,6},{8,9},{9,8},{10,11... | collective-permute-start | bytes 1843208 | tf_op jit(solution)/shard_map/ppermute | solution.py:205
  47.3 1.2 shard_map.97
  48.5 9.7 %all-to-all-start.1 = ((bf16[32,16,300]{2,1,0:T(8,128)(2,1)}), bf16[32,16,300]{2,1,0:T(8,128)(2,1)S(1)}, u32[]{:S(2)}, u32[]{:S(2)}) async-start(bf16[32,16,300]{2,1,0:T(8,128)(2,1)} %shard_map.97), calls=%async_computation.1 | async-start | bytes 786432 | tf_op jit(solution)/shard_map/all_to_all | solution.py:207
  58.3 0.9 shard_map.95
  62.1 10.6 %all-to-all-done.1.arrived_ref = bf16[32,16,300]{2,1,0:T(8,128)(2,1)S(1)} async-done(((bf16[32,16,300]{2,1,0:T(8,128)(2,1)}), bf16[32,16,300]{2,1,0:T(8,128)(2,1)S(1)}, u32[]{:S(2)}, u32[]{:S(2)}) %all-to-all-start.1) | async-done | bytes 307232 | tf_op jit(solution)/shard_map/all_to_all | solution.py:207
  72.7 0.9 copy-done.2
  73.6 0.9 copy-done.4
  74.6 0.9 copy-done.6
  75.5 0.8 copy-done.10
  76.4 0.8 copy-done.12
  77.2 10.7 %shard_map.98 = (f32[8,300,128]{2,1,0:T(8,128)S(1)}, f32[8,300,128]{2,1,0:T(8,128)S(1)}, f32[300,256]{1,0:T(8,128)S(1)}, bf16[32,16,300]{2,1,0:T(8,128)(2,1)}) custom-call(s32[1]{0:T(128)} %bitcast.core_ref, bf16[256,512]{1,0:T(8,128)(2,1)S(1)} %copy-done.2, bf16[512,256]{1,0:T(8,128)(2,1)S(1)} %copy-done.4, s32[512,128]{1,0:T(8,128)S(1)} %copy-done.6, ...), custom_call_target="tpu_custom_call" | custom-call | tf_op jit(solution)/shard_map/pallas_call | solution.py:225
  87.9 1.4 %copy.12 = f32[8,300,128]{2,0,1:T(8,128)} copy(f32[8,300,128]{2,1,0:T(8,128)S(1)} %get-tuple-element.17) | data formatting | bytes 2457600 | tf_op jit(solution)/shard_map/pallas_call | solution.py:225
  89.3 3.7 %collective-permute-start.1 = (f32[8,300,128]{2,0,1:T(8,128)}, f32[8,300,128]{2,0,1:T(8,128)S(1)}, u32[]{:S(2)}, u32[]{:S(2)}) collective-permute-start(f32[8,300,128]{2,0,1:T(8,128)} %copy.12), channel_id=1, source_target_pairs={{0,1},{1,0},{2,3},{3,2},{4,5},{5,4},{6,7},{7,6},{8,9},{9,8},{10,11... | collective-permute-start | bytes 3686408 | tf_op jit(solution)/shard_map/ppermute | solution.py:243
  93.1 4.0 %all-to-all-start.3 = ((bf16[32,16,300]{2,1,0:T(8,128)(2,1)}), bf16[32,16,300]{2,1,0:T(8,128)(2,1)S(1)}, u32[]{:S(2)}, u32[]{:S(2)}) async-start(bf16[32,16,300]{2,1,0:T(8,128)(2,1)} %get-tuple-element.19), calls=%async_computation.3 | async-start | bytes 786432 | tf_op jit(solution)/shard_map/all_to_all | solution.py:244
  97.1 1.1 fusion
  98.2 13.3 %all-to-all-done.3.returned_ref = bf16[32,16,300]{2,1,0:T(8,128)(2,1)S(1)} async-done(((bf16[32,16,300]{2,1,0:T(8,128)(2,1)}), bf16[32,16,300]{2,1,0:T(8,128)(2,1)S(1)}, u32[]{:S(2)}, u32[]{:S(2)}) %all-to-all-start.3) | async-done | bytes 307232 | tf_op jit(solution)/shard_map/all_to_all | solution.py:244
  111.5 5.2 %all-to-all-start.2 = ((bf16[8,300,128]{2,1,0:T(8,128)(2,1)}), bf16[8,300,128]{2,1,0:T(8,128)(2,1)S(1)}, u32[]{:S(2)}, u32[]{:S(2)}) async-start(bf16[8,300,128]{2,1,0:T(8,128)(2,1)} %fusion), calls=%async_computation.2 | async-start | bytes 1245184 | tf_op jit(solution)/shard_map/all_to_all | solution.py:246
  116.7 1.2 shard_map.99
  117.9 16.6 %all-to-all-done.2 = bf16[8,300,128]{2,1,0:T(8,128)(2,1)S(1)} async-done(((bf16[8,300,128]{2,1,0:T(8,128)(2,1)}), bf16[8,300,128]{2,1,0:T(8,128)(2,1)S(1)}, u32[]{:S(2)}, u32[]{:S(2)}) %all-to-all-start.2) | async-done | bytes 614432 | tf_op jit(solution)/shard_map/all_to_all | solution.py:246
  134.5 0.7 convert_reduce_fusion
  (38 shorter events, 3.8 us)
Async XLA Ops:
  0.6 46.6 %copy-start = (bf16[256,300]{0,1:T(8,128)(2,1)S(1)}, bf16[256,300]{0,1:T(8,128)(2,1)}, u32[]{:S(2)}) copy-start(bf16[256,300]{0,1:T(8,128)(2,1)} %param.13) | copy-start | bytes 460804
  0.6 0.7 copy-start.14
  1.4 0.7 copy-start.16
  3.0 44.3 %all-to-all-start = ((f32[32,1,128]{2,1,0:T(1,128)}), f32[32,1,128]{2,1,0:T(1,128)S(1)}, u32[]{:S(2)}, u32[]{:S(2)}) async-start(f32[32,1,128]{2,1,0:T(1,128)} %shard_map.96), calls=%async_computation | async-start | bytes 32768 | tf_op jit(solution)/shard_map/all_to_all | solution.py:203
  38.7 19.6 %copy-start.9 = (s32[2048,8]{0,1:T(8,128)S(1)}, s32[2048,8]{0,1:T(8,128)}, u32[]{:S(2)}) copy-start(s32[2048,8]{0,1:T(8,128)} %param.11) | copy-start | bytes 196612
  38.7 19.6 %copy-start.13 = (f32[2048]{0:T(1024)S(1)}, f32[2048]{0:T(1024)}, u32[]{:S(2)}) copy-start(f32[2048]{0:T(1024)} %param.9) | copy-start | bytes 24580
  38.7 19.6 %copy-start.15 = (s32[256]{0:T(256)S(1)}, s32[256]{0:T(256)}, u32[]{:S(2)}) copy-start(s32[256]{0:T(256)} %param.14) | copy-start | bytes 3076
  38.7 19.6 %copy-start.17 = (s32[256]{0:T(256)S(1)}, s32[256]{0:T(256)}, u32[]{:S(2)}) copy-start(s32[256]{0:T(256)} %param.15) | copy-start | bytes 3076
  38.8 19.6 %copy-start.18 = (f32[16]{0:T(128)S(1)}, f32[16]{0:T(128)}, u32[]{:S(2)}) copy-start(f32[16]{0:T(128)} %prop_ref.1) | copy-start | bytes 196
  38.9 23.1 %collective-permute-start = (bf16[8,300,128]{2,0,1:T(8,128)(2,1)S(1)}, bf16[8,300,128]{2,0,1:T(8,128)(2,1)S(1)}, u32[]{:S(2)}, u32[]{:S(2)}) collective-permute-start(bf16[8,300,128]{2,0,1:T(8,128)(2,1)S(1)} %copy.10), channel_id=1, source_target_pairs={{0,1},{1,0},{2,3},{3,2},{4,5},{5,4},{6,7},{7,6},{8,9},{9,8},{10,11... | collective-permute-start | bytes 1843208 | tf_op jit(solution)/shard_map/ppermute | solution.py:205
  47.2 12.1 %copy-start.7 = (f32[32,1,128]{2,1,0:T(1,128)}, f32[32,1,128]{2,1,0:T(1,128)S(1)}, u32[]{:S(2)}) copy-start(f32[32,1,128]{2,1,0:T(1,128)S(1)} %all-to-all-done.ask_ref) | copy-start | bytes 49156
  48.5 24.2 %all-to-all-start.1 = ((bf16[32,16,300]{2,1,0:T(8,128)(2,1)}), bf16[32,16,300]{2,1,0:T(8,128)(2,1)S(1)}, u32[]{:S(2)}, u32[]{:S(2)}) async-start(bf16[32,16,300]{2,1,0:T(8,128)(2,1)} %shard_map.97), calls=%async_computation.1 | async-start | bytes 786432 | tf_op jit(solution)/shard_map/all_to_all | solution.py:207
  59.3 0.7 copy-start.1
  60.0 0.7 copy-start.3
  60.7 0.7 copy-start.5
  72.7 1.0 copy-start.2
  73.6 0.9 copy-start.4
  74.6 0.9 copy-start.6
  75.5 0.8 copy-start.10
  76.4 0.8 copy-start.12
  89.3 7.7 %collective-permute-start.1 = (f32[8,300,128]{2,0,1:T(8,128)}, f32[8,300,128]{2,0,1:T(8,128)S(1)}, u32[]{:S(2)}, u32[]{:S(2)}) collective-permute-start(f32[8,300,128]{2,0,1:T(8,128)} %copy.12), channel_id=1, source_target_pairs={{0,1},{1,0},{2,3},{3,2},{4,5},{5,4},{6,7},{7,6},{8,9},{9,8},{10,11... | collective-permute-start | bytes 3686408 | tf_op jit(solution)/shard_map/ppermute | solution.py:243
  93.1 18.5 %all-to-all-start.3 = ((bf16[32,16,300]{2,1,0:T(8,128)(2,1)}), bf16[32,16,300]{2,1,0:T(8,128)(2,1)S(1)}, u32[]{:S(2)}, u32[]{:S(2)}) async-start(bf16[32,16,300]{2,1,0:T(8,128)(2,1)} %get-tuple-element.19), calls=%async_computation.3 | async-start | bytes 786432 | tf_op jit(solution)/shard_map/all_to_all | solution.py:244
  98.2 18.5 %copy-start.8 = (f32[32,1,128]{2,1,0:T(1,128)S(1)}, f32[32,1,128]{2,1,0:T(1,128)}, u32[]{:S(2)}) copy-start(f32[32,1,128]{2,1,0:T(1,128)} %copy-done.7) | copy-start | bytes 49156
  111.5 23.0 %all-to-all-start.2 = ((bf16[8,300,128]{2,1,0:T(8,128)(2,1)}), bf16[8,300,128]{2,1,0:T(8,128)(2,1)S(1)}, u32[]{:S(2)}, u32[]{:S(2)}) async-start(bf16[8,300,128]{2,1,0:T(8,128)(2,1)} %fusion), calls=%async_computation.2 | async-start | bytes 1245184 | tf_op jit(solution)/shard_map/all_to_all | solution.py:246
  (1 other events, 0.6 us)

commit v2 on v1

v2 whole, which is shorter than its diff:
```python
import jax
import jax.numpy as jnp
from jax import lax
from jax.experimental import pallas as pl
from jax.experimental.pallas import tpu as pltpu
from jax.sharding import PartitionSpec as P

BF16 = jnp.bfloat16
F32 = jnp.float32
I32 = jnp.int32
LANES = 128
CAP = 16
ROW_CHUNK = 32
BIG = 60

VMEM = pl.BlockSpec(memory_space=pltpu.VMEM)
SMEM = pl.BlockSpec(memory_space=pltpu.SMEM)
ANY = pl.BlockSpec(memory_space=pl.ANY)

HOPS = ((4, 1, 7, 0), (3, 5, 2, 6))


def iota(shape, dim):
    return lax.broadcasted_iota(I32, shape, dim)


def ones(mask):
    return jnp.where(mask, 1.0, 0.0).astype(BF16)


def nt(a, b):
    return lax.dot_general(a, b, (((1,), (1,)), ((), ())), preferred_element_type=F32)


def nn(a, b):
    return lax.dot_general(a, b, (((1,), (0,)), ((), ())), preferred_element_type=F32)


def tn(a, b):
    return lax.dot_general(a, b, (((0,), (0,)), ((), ())), preferred_element_type=F32)


def call(kernel, out, ins, scratch=(), vmem=8, outs=None):
    return pl.pallas_call(
        kernel,
        out_shape=out,
        in_specs=ins,
        out_specs=outs or jax.tree.map(lambda _: VMEM, out),
        scratch_shapes=scratch,
        compiler_params=pltpu.CompilerParams(vmem_limit_bytes=vmem * 2**20),
    )


def hops(chips, k, way):
    return [(2 * y + c, 2 * ((y + way * HOPS[c][k]) % chips) + c) for y in range(chips) for c in range(2)]


def after(values, *earlier):
    return lax.optimization_barrier((*values, *earlier))[:len(values)]


def fetch(sems, *moves):
    copies = [pltpu.make_async_copy(src, dst, sems.at[i]) for i, (src, dst) in enumerate(moves)]
    for copy in copies:
        copy.start()
    return copies


def wait(copies):
    for copy in copies:
        copy.wait()


def ranks(owner, sections):
    n = owner.shape[1]
    hot = owner == iota((sections, n), 0)
    upper = ones(iota((n, n), 0) < iota((n, n), 1))
    before = nn(ones(hot), upper)
    return hot, jnp.sum(jnp.where(hot, before, 0.0), axis=0, keepdims=True)


def pad_kernel(qt_hbm, wt_hbm, qp_ref, wp_ref, qt_ref, wt_ref, sems):
    copies = fetch(sems, (qt_hbm, qt_ref), (wt_hbm, wt_ref))
    dim = qt_hbm.shape[0]
    for copy, src, dst in zip(copies, (qt_ref, wt_ref), (qp_ref, wp_ref)):
        copy.wait()
        dst[:dim, :] = src[...]
        dst[dim:, :] = jnp.zeros((dst.shape[0] - dim, dst.shape[1]), dst.dtype)


def ask_kernel(owner_hbm, row_hbm, ask_ref, owner_ref, row_ref, sems):
    wait(fetch(sems, (owner_hbm, owner_ref), (row_hbm, row_ref)))
    sections = ask_ref.shape[0]
    owner = owner_ref[...]
    hot, rank = ranks(owner, sections)
    rows = jnp.where(hot, row_ref[...].astype(F32) + 1.0, 0.0).astype(BF16)
    place = ones(iota((LANES, owner.shape[1]), 0).astype(F32) == rank)
    ask_ref[...] = jnp.broadcast_to(nt(rows, place)[:, None, :], ask_ref.shape)


def wanted_hot(ask, prim):
    sections = ask.shape[0]
    places = sections * CAP
    spread = ones(iota((places, sections), 0) // CAP == iota((places, sections), 1))
    every = nn(spread, ask.astype(BF16))
    mine = iota((places, LANES), 0) % CAP == iota((places, LANES), 1)
    column = jnp.sum(jnp.where(mine, every, 0.0), axis=1, keepdims=True)
    return ones(iota((places, prim), 1).astype(F32) + 1.0 == column)


def serve_kernel(ask_ref, wt_ref, served_ref):
    ask = ask_ref[:, 0, :]
    hot = wanted_hot(ask, wt_ref.shape[1])
    served_ref[...] = nt(hot, wt_ref[...]).astype(BF16).reshape(served_ref.shape)


def prepare_kernel(
    first_ref, prop_ref, owner_ref, row_ref, wt_ref, bucket_ref, weight_ref,
    comp_ref, comp_t_ref, slots_ref, wrow_ref, value_ref,
):
    sections = comp_ref.shape[1] // CAP
    owner = owner_ref[...]
    prim = wt_ref.shape[1]
    n = owner.shape[1]
    _, rank = ranks(owner, sections)
    target = owner.astype(F32) * CAP + rank
    places = sections * CAP
    comp_t_ref[...] = ones(iota((places, n), 0).astype(F32) == target)
    target_col = jnp.broadcast_to(target, (LANES, n)).T
    for block in range(places // LANES):
        comp_ref[:, block * LANES:(block + 1) * LANES] = ones(
            (iota((n, LANES), 1) + block * LANES).astype(F32) == target_col
        )
    first = first_ref[0]
    leaf_base = first_ref[1]
    stride = first_ref[2]
    slots_ref[:prim, :] = iota((prim, LANES), 0) + first
    label = owner * stride + leaf_base + row_ref[...]
    slots_ref[prim:, :] = jnp.broadcast_to(label, (LANES, n)).T
    wrow_ref[...] = (wt_ref[...].astype(F32).T * 0.5).astype(BF16)
    bucket = bucket_ref[...]
    value = jnp.zeros(bucket.shape, F32)
    for b in range(prop_ref.shape[0]):
        value = jnp.where(bucket == b, prop_ref[b], value)
    value_ref[...] = value * weight_ref[...] * 0.5


def grad_kernel(
    columns_ref, arrived_hbm, q0_hbm, q1_hbm, q2_hbm, q3_hbm, sib_hbm,
    comp_hbm, comp_t_hbm, slots_hbm, wrow_hbm, wt_hbm, label_hbm, value_hbm, weight_hbm,
    part_sib_hbm, part_own_hbm, prim_hbm, back_ref,
    arrived_ref, sib_ref, own_ref, comp_ref, comp_t_ref, slots_ref, w_scr, wt_scr, label_ref, value_ref, weight_ref,
    part_ref, prim_ref, logit_scr, coef_scr, copy_scr, in_sems, out_sems,
):
    prim = wt_hbm.shape[1]
    slots = slots_ref.shape[0]
    dim = wt_hbm.shape[0]
    copies = fetch(
        in_sems,
        (arrived_hbm, arrived_ref),
        (comp_hbm, comp_ref),
        (wrow_hbm, w_scr.at[:prim, :]),
        (wt_hbm, wt_scr.at[:, :prim]),
        (sib_hbm, sib_ref),
        (slots_hbm, slots_ref),
        (label_hbm, label_ref),
        (value_hbm, value_ref),
        (weight_hbm, weight_ref),
        (q0_hbm, own_ref.at[0:2]),
        (q1_hbm, own_ref.at[2:4]),
        (q2_hbm, own_ref.at[4:6]),
        (q3_hbm, own_ref.at[6:8]),
        (comp_t_hbm, comp_t_ref),
    )
    prim_ref[...] = jnp.zeros(prim_ref.shape, F32)
    copy_scr[...] = jnp.zeros(copy_scr.shape, F32)
    wait(copies[:2])
    fetched = nn(comp_ref[...], arrived_ref[...].reshape(-1, dim))
    w_scr[prim:, :] = (fetched * 0.5).astype(BF16)
    wt_scr[:, prim:] = fetched.T.astype(BF16)
    wait(copies[2:])

    def pair(q, k):
        logit_scr[...] = nn(w_scr[...], q)
        for side in range(2):
            at = pl.ds(pl.multiple_of(columns_ref[2 * k + side] * LANES, LANES), LANES)
            half_weight = weight_ref[:, at] * 0.5
            labels = label_ref[:, at]
            values = value_ref[:, at]
            lanes = slice(side * LANES, (side + 1) * LANES)
            for r in range(0, slots, ROW_CHUNK):
                rows = slice(r, r + ROW_CHUNK)
                t = jnp.tanh(logit_scr[rows, lanes])
                slot = slots_ref[rows, :]
                total = jnp.where(slot == labels[0:1, :], values[0:1, :], 0.0)
                for p in range(1, labels.shape[0]):
                    total = total + jnp.where(slot == labels[p:p + 1, :], values[p:p + 1, :], 0.0)
                hit = total > 0.0
                scale = jnp.where(hit, total, half_weight)
                coef_scr[rows, lanes] = (scale * (t + jnp.where(hit, -1.0, 1.0))).astype(BF16)
        coef = coef_scr[...]
        prim_ref[...] += nt(q, coef[:prim])
        copy_scr[...] += nt(coef[prim:], q)
        return nn(wt_scr[...], coef)

    chips = sib_ref.shape[0] // 2

    def step(k, carry):
        sib = k < chips
        at = 2 * jnp.where(sib, k, k - chips)

        def run(q_ref, out_hbm):
            part = pair(jnp.concatenate([q_ref[at], q_ref[at + 1]], axis=1), jnp.where(sib, k + chips, k - chips))
            part_ref[2 * k] = part[:, :LANES]
            part_ref[2 * k + 1] = part[:, LANES:]
            pltpu.make_async_copy(part_ref.at[pl.ds(2 * k, 2)], out_hbm.at[pl.ds(at, 2)], out_sems.at[k]).start()

        pl.when(sib)(lambda: run(sib_ref, part_sib_hbm))
        pl.when(jnp.logical_not(sib))(lambda: run(own_ref, part_own_hbm))
        return carry

    lax.fori_loop(0, 2 * chips, step, 0)
    last = pltpu.make_async_copy(prim_ref, prim_hbm, out_sems.at[2 * chips])
    last.start()
    back = nn(comp_t_ref[...], copy_scr[...].astype(BF16))
    back_ref[...] = back.astype(BF16).reshape(back_ref.shape)
    for k in range(2 * chips):
        out_hbm = part_sib_hbm if k < chips else part_own_hbm
        at = 2 * (k % chips)
        pltpu.make_async_copy(part_ref.at[2 * k:2 * k + 2], out_hbm.at[at:at + 2], out_sems.at[k]).wait()
    last.wait()


def finish_kernel(ask_ref, prim_ref, returned_ref, out_ref):
    ask = ask_ref[:, 0, :]
    hot = wanted_hot(ask, prim_ref.shape[1])
    returned = returned_ref[...].reshape(-1, prim_ref.shape[0])
    out_ref[...] = (prim_ref[...] + tn(returned, hot))[:out_ref.shape[0]]


def on_device(
    query_feats, query_weight, positive_label, positive_bucket, inv_prop, primary_w, copy_owner, copy_row
):
    sections = lax.axis_size("section")
    leaves = lax.axis_size("leaf")
    section_id = lax.axis_index("section")
    leaf_id = lax.axis_index("leaf")
    prim, features = primary_w.shape
    n = copy_owner.shape[0]
    slots = prim + n
    chips = leaves // 2
    sibling = [(i, i ^ 1) for i in range(leaves)]
    queries = query_feats.shape[0]
    shape = jax.ShapeDtypeStruct

    owner = copy_owner.reshape(1, n)
    row = copy_row.reshape(1, n)
    dim = 16 * pl.cdiv(features, 16)

    ask = call(
        ask_kernel,
        shape((sections, 8, LANES), F32),
        [ANY] * 2,
        scratch=(pltpu.VMEM((1, n), I32), pltpu.VMEM((1, n), I32), pltpu.SemaphoreType.DMA((2,))),
        vmem=BIG,
    )(owner, row)
    wanted = lax.all_to_all(ask, "section", split_axis=0, concat_axis=0, tiled=True)
    qp, wp = call(
        pad_kernel,
        (shape((dim, queries), BF16), shape((dim, prim), BF16)),
        [ANY] * 2,
        scratch=(
            pltpu.VMEM((features, queries), BF16),
            pltpu.VMEM((features, prim), BF16),
            pltpu.SemaphoreType.DMA((2,)),
        ),
        vmem=BIG,
    )(*after((query_feats.T, primary_w.T), ask))
    both = jnp.stack([qp, lax.ppermute(qp, "leaf", sibling)])
    own = [lax.ppermute(both, "leaf", hops(chips, k, 1)) for k in range(4)]
    served = call(serve_kernel, shape((sections, CAP, dim), BF16), [VMEM] * 2)(wanted, wp)
    own = after(own, served)
    sib = lax.ppermute(jnp.concatenate(own), "leaf", sibling)
    arrived = lax.all_to_all(served, "section", split_axis=0, concat_axis=0, tiled=True)

    first = (section_id * leaves + leaf_id) * prim
    numbers = jnp.stack([first, leaf_id * prim, jnp.int32(leaves * prim)]).astype(I32)
    weight = query_weight.reshape(1, -1)
    comp, comp_t, slot_ids, wrow, value = call(
        prepare_kernel,
        (
            shape((n, sections * CAP), BF16),
            shape((sections * CAP, n), BF16),
            shape((slots, LANES), I32),
            shape((prim, dim), BF16),
            shape(positive_label.shape[::-1], F32),
        ),
        [SMEM, SMEM] + [VMEM] * 5,
        vmem=BIG,
    )(numbers, inv_prop, owner, row, wp, positive_bucket.T, weight)

    core = leaf_id % 2
    chip = leaf_id // 2
    near = jnp.array(HOPS, I32)
    mine = (chip - near[core]) % chips
    other = (chip - near[1 - core]) % chips
    ends = jnp.stack([core, 1 - core])
    columns = jnp.concatenate(
        [(2 * mine[:, None] + ends[None, :]).reshape(-1), (2 * other[:, None] + ends[None, ::-1]).reshape(-1)]
    ).astype(I32)
    total = positive_label.shape[0]
    part_sib, part_own, prim_t, back = call(
        grad_kernel,
        (
            shape((chips, dim, queries), F32),
            shape((chips, dim, queries), F32),
            shape((dim, prim), F32),
            shape((sections, CAP, dim), BF16),
        ),
        [SMEM] + [ANY] * 14,
        scratch=(
            pltpu.VMEM(arrived.shape, BF16),
            pltpu.VMEM(sib.shape, BF16),
            pltpu.VMEM(sib.shape, BF16),
            pltpu.VMEM(comp.shape, BF16),
            pltpu.VMEM(comp_t.shape, BF16),
            pltpu.VMEM((slots, LANES), I32),
            pltpu.VMEM((slots, dim), BF16),
            pltpu.VMEM((dim, slots), BF16),
            pltpu.VMEM((positive_label.shape[1], total), I32),
            pltpu.VMEM((positive_label.shape[1], total), F32),
            pltpu.VMEM((1, total), F32),
            pltpu.VMEM((leaves, dim, queries), F32),
            pltpu.VMEM((dim, prim), F32),
            pltpu.VMEM((slots, 2 * LANES), F32),
            pltpu.VMEM((slots, 2 * LANES), BF16),
            pltpu.VMEM((n, dim), F32),
            pltpu.SemaphoreType.DMA((14,)),
            pltpu.SemaphoreType.DMA((chips + 1,)),
        ),
        vmem=BIG,
        outs=(ANY, ANY, ANY, VMEM),
    )(columns, arrived, *own, sib, comp, comp_t, slot_ids, wrow, wp, positive_label.T, value, weight)

    swapped = lax.ppermute(part_sib, "leaf", sibling)
    returned = lax.all_to_all(back, "section", split_axis=0, concat_axis=0, tiled=True)
    sums = (part_own + swapped).astype(BF16)
    pieces = [lax.ppermute(sums[2 * k:2 * k + 2], "leaf", hops(chips, k, -1)) for k in range(4)]
    prim_grad = call(finish_kernel, shape((features, prim), F32), [VMEM] * 3)(wanted, prim_t, returned)
    pieces = after(pieces, prim_grad)
    gathered = sum(piece.astype(F32) for piece in pieces)
    query_grad = gathered[0] + lax.ppermute(gathered[1], "leaf", sibling)
    return query_grad[:features].T, prim_grad.T


def solution(mesh):
    placed = (
        P(("section", "leaf"), None),
        P("section"),
        P("section", None),
        P("section", None),
        P(),
        P(("section", "leaf"), None),
        P(("section", "leaf")),
        P(("section", "leaf")),
    )
    return jax.shard_map(
        on_device,
        mesh=mesh,
        in_specs=placed,
        out_specs=(P(("section", "leaf"), None), P(("section", "leaf"), None)),
        check_vma=False,
    )
```

time: 137 us -> 113 us (0.82)
  waiting for transfers between devices: 40.5 us -> 15.7 us
  starting transfers between devices: 44.6 us -> 67.9 us
  blocking collectives: 22 us -> 0 us
  local copies, waits for them, and re-layouts: 10.3 us -> 2.17 us
  Pallas kernels: 15 us -> 21 us
  other arithmetic: 1.93 us -> 4.56 us
    ppermute x2 -> x12, starting transfers between devices: 12 us -> 47.1 us  [the longest x4 15.8 us: on_device(): lax.ppermute(sums[2 * k:2 * k + 2], 'leaf', hops(chips, k, -1))]
    all_gather x1 -> x0, blocking collectives: 22 us -> none  [on_device(): lax.all_gather(qt, 'leaf', axis=0, tiled=False, axis_index_groups=same_core)]
    all_to_all x1 -> x0, waiting for transfers between devices: 16.6 us -> none  [on_device(): lax.all_to_all(pair, 'leaf', split_axis=0, concat_axis=0, axis_index_grou...]
    all_to_all x1, waiting for transfers between devices: 13.3 us -> 0.01 us  [on_device(): lax.all_to_all(back, 'section', split_axis=0, concat_axis=0, tiled=True)]
    ppermute x2 -> x12, waiting for transfers between devices: 0.01 us -> 7.34 us  [the longest x4 5.97 us: on_device(): lax.ppermute(sums[2 * k:2 * k + 2], 'leaf', hops(chips, k, -1))]
    unnamed x38 -> x18, local copies, waits for them, and re-layouts: 8.68 us -> 1.84 us
    all_to_all x1, starting transfers between devices: 13.7 us -> 7.52 us  [on_device(): lax.all_to_all(ask, 'section', split_axis=0, concat_axis=0, tiled=True)]
    all_to_all x1 -> x0, starting transfers between devices: 5.18 us -> none  [on_device(): lax.all_to_all(pair, 'leaf', split_axis=0, concat_axis=0, axis_index_grou...]
  transfers between devices with their start and end apart: 6 -> 15, of which waited for: 3 -> 4; matrix products, arithmetic and copies ran while one was open for 1% -> 4% of each run, Pallas kernels for 3% -> 4%
where the time goes in v2:
time: 113 us; the launch traced here: 112 us
  starting transfers between devices  67.9 us (60%)
  Pallas kernels  21 us (19%)
  waiting for transfers between devices  15.7 us (14%)
  other arithmetic  4.56 us (4%)
  local copies, waits for them, and re-layouts  2.17 us (2%)
    ppermute x4, starting transfers between devices, on_device(): lax.ppermute(sums[2 * k:2 * k + 2], 'leaf', hops(chips, k, -1))  15.8 us
    ppermute x4, starting transfers between devices, on_device(): own = [lax.ppermute(both, 'leaf', hops(chips, k, 1)) for k in range(4)]  14.9 us
    pallas_call x1, Pallas kernels, on_device(): call(grad_kernel, (shape((chips, dim, queries), F32), shape((chips, dim,...  13 us
    all_to_all x1, starting transfers between devices, on_device(): lax.all_to_all(served, 'section', split_axis=0, concat_axis=0, tiled=True)  9.22 us
    ppermute x1, starting transfers between devices, on_device(): both = jnp.stack([qp, lax.ppermute(qp, 'leaf', sibling)])  8.79 us
    all_to_all x1, waiting for transfers between devices, on_device(): lax.all_to_all(served, 'section', split_axis=0, concat_axis=0, tiled=True)  8.4 us
    all_to_all x1, starting transfers between devices, on_device(): lax.all_to_all(ask, 'section', split_axis=0, concat_axis=0, tiled=True)  7.52 us
    ppermute x4, waiting for transfers between devices, on_device(): lax.ppermute(sums[2 * k:2 * k + 2], 'leaf', hops(chips, k, -1))  5.97 us
  transfers between devices with their start and end apart: 15, of which 4 were waited for; matrix products, arithmetic and copies ran while one was open for 4% of the time, Pallas kernels for 4%

profile of v2, /device:TPU:1, one launch (start us, length us, event | category | flops | bytes accessed | tf_op | source)
XLA Modules:
  0.0 112.4 jit_solution(13215098859474567252)
XLA Ops:
  0.6 1.7 %shard_map.104 = f32[32,8,128]{2,1,0:T(8,128)} custom-call(s32[1,256]{1,0:T(1,128)} %bitcast.33, s32[1,256]{1,0:T(1,128)} %bitcast.35), custom_call_target="tpu_custom_call" | custom-call | tf_op jit(solution)/shard_map/pallas_call | solution.py:260
  2.3 1.7 %shard_map.105 = (bf16[304,128]{1,0:T(8,128)(2,1)}, bf16[304,256]{1,0:T(8,128)(2,1)}) custom-call(bf16[300,128]{1,0:T(8,128)(2,1)} %bitcast.26, bf16[300,256]{1,0:T(8,128)(2,1)} %bitcast.25), custom_call_target="tpu_custom_call" | custom-call | tf_op jit(solution)/shard_map/pallas_call | solution.py:268
  4.0 8.8 %collective-permute-start = (bf16[304,128]{1,0:T(8,128)(2,1)}, bf16[304,128]{1,0:T(8,128)(2,1)S(1)}, u32[]{:S(2)}, u32[]{:S(2)}) collective-permute-start(bf16[304,128]{1,0:T(8,128)(2,1)} %get-tuple-element.26), channel_id=1, source_target_pairs={{0,1},{1,0},{2,3},{3,2},{4,5},{5,4},{6,7},{7,6},{8,9},{9,8},{10,11... | collective-permute-start | bytes 233480 | tf_op jit(solution)/shard_map/ppermute | solution.py:279
  12.8 7.5 %all-to-all-start = ((f32[32,8,128]{2,1,0:T(8,128)}), f32[32,8,128]{2,1,0:T(8,128)S(1)}, u32[]{:S(2)}, u32[]{:S(2)}) async-start(f32[32,8,128]{2,1,0:T(8,128)} %shard_map.104), calls=%async_computation | async-start | bytes 262144 | tf_op jit(solution)/shard_map/all_to_all | solution.py:267
  21.2 5.9 %collective-permute-start.4 = (bf16[2,304,128]{2,1,0:T(8,128)(2,1)S(1)}, bf16[2,304,128]{2,1,0:T(8,128)(2,1)S(1)}, u32[]{:S(2)}, u32[]{:S(2)}) collective-permute-start(bf16[2,304,128]{2,1,0:T(8,128)(2,1)S(1)} %pad_maximum_fusion.1), channel_id=1, source_target_pairs={{0,0},{1,13},{2,2},{3,15},{4,4},{5,1},{6,6},{7,3},{8,8},{9,5},{10,... | collective-permute-start | bytes 466952 | tf_op jit(solution)/shard_map/ppermute | solution.py:280
  27.1 1.9 %collective-permute-start.3 = (bf16[2,304,128]{2,1,0:T(8,128)(2,1)S(1)}, bf16[2,304,128]{2,1,0:T(8,128)(2,1)S(1)}, u32[]{:S(2)}, u32[]{:S(2)}) collective-permute-start(bf16[2,304,128]{2,1,0:T(8,128)(2,1)S(1)} %pad_maximum_fusion.1), channel_id=1, source_target_pairs={{0,14},{1,5},{2,0},{3,7},{4,2},{5,9},{6,4},{7,11},{8,6},{9,13},{10... | collective-permute-start | bytes 466952 | tf_op jit(solution)/shard_map/ppermute | solution.py:280
  29.1 5.0 %collective-permute-start.2 = (bf16[2,304,128]{2,1,0:T(8,128)(2,1)S(1)}, bf16[2,304,128]{2,1,0:T(8,128)(2,1)S(1)}, u32[]{:S(2)}, u32[]{:S(2)}) collective-permute-start(bf16[2,304,128]{2,1,0:T(8,128)(2,1)S(1)} %pad_maximum_fusion.1), channel_id=1, source_target_pairs={{0,2},{1,11},{2,4},{3,13},{4,6},{5,15},{6,8},{7,1},{8,10},{9,3},{1... | collective-permute-start | bytes 466952 | tf_op jit(solution)/shard_map/ppermute | solution.py:280
  34.1 2.0 %collective-permute-start.1 = (bf16[2,304,128]{2,1,0:T(8,128)(2,1)S(1)}, bf16[2,304,128]{2,1,0:T(8,128)(2,1)S(1)}, u32[]{:S(2)}, u32[]{:S(2)}) collective-permute-start(bf16[2,304,128]{2,1,0:T(8,128)(2,1)S(1)} %pad_maximum_fusion.1), channel_id=1, source_target_pairs={{0,8},{1,7},{2,10},{3,9},{4,12},{5,11},{6,14},{7,13},{8,0},{9,15},... | collective-permute-start | bytes 466952 | tf_op jit(solution)/shard_map/ppermute | solution.py:280
  38.3 9.2 %all-to-all-start.1 = ((bf16[32,16,304]{2,1,0:T(8,128)(2,1)}), bf16[32,16,304]{2,1,0:T(8,128)(2,1)S(1)}, u32[]{:S(2)}, u32[]{:S(2)}) async-start(bf16[32,16,304]{2,1,0:T(8,128)(2,1)} %shard_map.106), calls=%async_computation.1 | async-start | bytes 786432 | tf_op jit(solution)/shard_map/all_to_all | solution.py:284
  47.7 2.1 %collective-permute-start.5 = (bf16[8,304,128]{2,1,0:T(8,128)(2,1)S(1)}, bf16[8,304,128]{2,1,0:T(8,128)(2,1)S(1)}, u32[]{:S(2)}, u32[]{:S(2)}) collective-permute-start(bf16[8,304,128]{2,1,0:T(8,128)(2,1)S(1)} %pad_maximum_fusion), channel_id=1, source_target_pairs={{0,1},{1,0},{2,3},{3,2},{4,5},{5,4},{6,7},{7,6},{8,9},{9,8},{10,11... | collective-permute-start | bytes 1867784 | tf_op jit(solution)/shard_map/ppermute | solution.py:283
  51.0 2.2 %shard_map.107 = (bf16[256,512]{1,0:T(8,128)(2,1)}, bf16[512,256]{1,0:T(8,128)(2,1)}, s32[512,128]{1,0:T(8,128)}, bf16[256,304]{1,0:T(8,128)(2,1)}, f32[8,2048]{1,0:T(8,128)}) custom-call(s32[3]{0:T(128)} %pad_add_fusion.2.first_ref, f32[16]{0:T(128)} %prop_ref.1, s32[1,256]{1,0:T(1,128)} %bitcast.34, s32[1,256]{1,0:T(1,128)} %bitcast.36, ...), custom_call_target="tpu_custom_call" | custom-call | tf_op jit(solution)/shard_map/pallas_call | solution.py:289
  53.7 8.4 %all-to-all-done.1.arrived_hbm = bf16[32,16,304]{2,1,0:T(8,128)(2,1)S(1)} async-done(((bf16[32,16,304]{2,1,0:T(8,128)(2,1)}), bf16[32,16,304]{2,1,0:T(8,128)(2,1)S(1)}, u32[]{:S(2)}, u32[]{:S(2)}) %all-to-all-start.1) | async-done | bytes 311328 | tf_op jit(solution)/shard_map/all_to_all | solution.py:284
  63.0 13.0 %shard_map.108 = (f32[8,304,128]{2,1,0:T(8,128)}, f32[8,304,128]{2,1,0:T(8,128)}, f32[304,256]{1,0:T(8,128)}, bf16[32,16,304]{2,1,0:T(8,128)(2,1)}) custom-call(s32[16]{0:T(128)} %pad_add_fusion.1.columns_ref, bf16[32,16,304]{2,1,0:T(8,128)(2,1)} %copy-done.2, bf16[2,304,128]{2,1,0:T(8,128)(2,1)} %copy-done.6, bf16[2,304,128]{2,1,0:T(8,128)(2,1)} %copy-done.5, ...), custom_call_target="tpu_custom_call" | custom-call | tf_op jit(solution)/shard_map/pallas_call | solution.py:312
  76.1 3.6 %collective-permute-start.6 = (f32[8,304,128]{2,1,0:T(8,128)}, f32[8,304,128]{2,1,0:T(8,128)S(1)}, u32[]{:S(2)}, u32[]{:S(2)}) collective-permute-start(f32[8,304,128]{2,1,0:T(8,128)} %get-tuple-element.37), channel_id=1, source_target_pairs={{0,1},{1,0},{2,3},{3,2},{4,5},{5,4},{6,7},{7,6},{8,9},{9,8},{10,11... | collective-permute-start | bytes 3735560 | tf_op jit(solution)/shard_map/ppermute | solution.py:345
  79.7 4.0 %all-to-all-start.2 = ((bf16[32,16,304]{2,1,0:T(8,128)(2,1)}), bf16[32,16,304]{2,1,0:T(8,128)(2,1)S(1)}, u32[]{:S(2)}, u32[]{:S(2)}) async-start(bf16[32,16,304]{2,1,0:T(8,128)(2,1)} %get-tuple-element.39), calls=%async_computation.2 | async-start | bytes 786432 | tf_op jit(solution)/shard_map/all_to_all | solution.py:346
  83.8 1.4 %add_convert_fusion = bf16[8,304,128]{2,1,0:T(8,128)(2,1)S(1)} fusion(f32[8,304,128]{2,1,0:T(8,128)} %get-tuple-element.36, f32[8,304,128]{2,1,0:T(8,128)S(1)} %collective-permute-done.6), kind=kLoop, calls=%fused_computation | loop fusion | flops 622592 | bytes 3112960 | tf_op jit(solution)/shard_map/convert_element_type | solution.py:347
  85.3 2.6 %collective-permute-start.10 = (bf16[2,304,128]{2,1,0:T(8,128)(2,1)S(1)}, bf16[2,304,128]{2,1,0:T(8,128)(2,1)S(1)}, u32[]{:S(2)}, u32[]{:S(2)}) collective-permute-start(bf16[2,304,128]{2,1,0:T(8,128)(2,1)S(1)} %get-tuple-element.44), channel_id=1, source_target_pairs={{0,0},{1,5},{2,2},{3,7},{4,4},{5,9},{6,6},{7,11},{8,8},{9,13},{10,... | collective-permute-start | bytes 466952 | tf_op jit(solution)/shard_map/ppermute | solution.py:348
  87.8 5.0 %collective-permute-start.9 = (bf16[2,304,128]{2,1,0:T(8,128)(2,1)S(1)}, bf16[2,304,128]{2,1,0:T(8,128)(2,1)S(1)}, u32[]{:S(2)}, u32[]{:S(2)}) collective-permute-start(bf16[2,304,128]{2,1,0:T(8,128)(2,1)S(1)} %get-tuple-element.45), channel_id=1, source_target_pairs={{0,2},{1,13},{2,4},{3,15},{4,6},{5,1},{6,8},{7,3},{8,10},{9,5},{10... | collective-permute-start | bytes 466952 | tf_op jit(solution)/shard_map/ppermute | solution.py:348
  92.8 2.5 %collective-permute-start.8 = (bf16[2,304,128]{2,1,0:T(8,128)(2,1)S(1)}, bf16[2,304,128]{2,1,0:T(8,128)(2,1)S(1)}, u32[]{:S(2)}, u32[]{:S(2)}) collective-permute-start(bf16[2,304,128]{2,1,0:T(8,128)(2,1)S(1)} %get-tuple-element.46), channel_id=1, source_target_pairs={{0,14},{1,7},{2,0},{3,9},{4,2},{5,11},{6,4},{7,13},{8,6},{9,15},{1... | collective-permute-start | bytes 466952 | tf_op jit(solution)/shard_map/ppermute | solution.py:348
  95.3 5.8 %collective-permute-start.7 = (bf16[2,304,128]{2,1,0:T(8,128)(2,1)S(1)}, bf16[2,304,128]{2,1,0:T(8,128)(2,1)S(1)}, u32[]{:S(2)}, u32[]{:S(2)}) collective-permute-start(bf16[2,304,128]{2,1,0:T(8,128)(2,1)S(1)} %get-tuple-element.47), channel_id=1, source_target_pairs={{0,8},{1,11},{2,10},{3,13},{4,12},{5,15},{6,14},{7,1},{8,0},{9,3},... | collective-permute-start | bytes 466952 | tf_op jit(solution)/shard_map/ppermute | solution.py:348
  102.4 3.2 %collective-permute-done.8 = bf16[2,304,128]{2,1,0:T(8,128)(2,1)S(1)} collective-permute-done((bf16[2,304,128]{2,1,0:T(8,128)(2,1)S(1)}, bf16[2,304,128]{2,1,0:T(8,128)(2,1)S(1)}, u32[]{:S(2)}, u32[]{:S(2)}) %collective-permute-start.8) | collective-permute-done | bytes 155680 | tf_op jit(solution)/shard_map/ppermute | solution.py:348
  105.5 2.8 %collective-permute-done.7 = bf16[2,304,128]{2,1,0:T(8,128)(2,1)S(1)} collective-permute-done((bf16[2,304,128]{2,1,0:T(8,128)(2,1)S(1)}, bf16[2,304,128]{2,1,0:T(8,128)(2,1)S(1)}, u32[]{:S(2)}, u32[]{:S(2)}) %collective-permute-start.7) | collective-permute-done | bytes 155680 | tf_op jit(solution)/shard_map/ppermute | solution.py:348
  108.4 1.9 %collective-permute-start.11 = (f32[304,128]{1,0:T(8,128)S(1)}, f32[304,128]{1,0:T(8,128)S(1)}, u32[]{:S(2)}, u32[]{:S(2)}) collective-permute-start(f32[304,128]{1,0:T(8,128)S(1)} %get-tuple-element.49), channel_id=1, source_target_pairs={{0,1},{1,0},{2,3},{3,2},{4,5},{5,4},{6,7},{7,6},{8,9},{9,8},{10,11... | collective-permute-start | bytes 466952 | tf_op jit(solution)/shard_map/ppermute | solution.py:352
  110.4 1.3 %collective-permute-done.11 = f32[304,128]{1,0:T(8,128)S(1)} collective-permute-done((f32[304,128]{1,0:T(8,128)S(1)}, f32[304,128]{1,0:T(8,128)S(1)}, u32[]{:S(2)}, u32[]{:S(2)}) %collective-permute-start.11) | collective-permute-done | bytes 155680 | tf_op jit(solution)/shard_map/ppermute | solution.py:352
  (45 shorter events, 7.8 us)
Async XLA Ops:
  4.0 16.3 %collective-permute-start = (bf16[304,128]{1,0:T(8,128)(2,1)}, bf16[304,128]{1,0:T(8,128)(2,1)S(1)}, u32[]{:S(2)}, u32[]{:S(2)}) collective-permute-start(bf16[304,128]{1,0:T(8,128)(2,1)} %get-tuple-element.26), channel_id=1, source_target_pairs={{0,1},{1,0},{2,3},{3,2},{4,5},{5,4},{6,7},{7,6},{8,9},{9,8},{10,11... | collective-permute-start | bytes 233480 | tf_op jit(solution)/shard_map/ppermute | solution.py:279
  12.8 23.4 %all-to-all-start = ((f32[32,8,128]{2,1,0:T(8,128)}), f32[32,8,128]{2,1,0:T(8,128)S(1)}, u32[]{:S(2)}, u32[]{:S(2)}) async-start(f32[32,8,128]{2,1,0:T(8,128)} %shard_map.104), calls=%async_computation | async-start | bytes 262144 | tf_op jit(solution)/shard_map/all_to_all | solution.py:267
  21.2 26.3 %collective-permute-start.4 = (bf16[2,304,128]{2,1,0:T(8,128)(2,1)S(1)}, bf16[2,304,128]{2,1,0:T(8,128)(2,1)S(1)}, u32[]{:S(2)}, u32[]{:S(2)}) collective-permute-start(bf16[2,304,128]{2,1,0:T(8,128)(2,1)S(1)} %pad_maximum_fusion.1), channel_id=1, source_target_pairs={{0,0},{1,13},{2,2},{3,15},{4,4},{5,1},{6,6},{7,3},{8,8},{9,5},{10,... | collective-permute-start | bytes 466952 | tf_op jit(solution)/shard_map/ppermute | solution.py:280
  27.1 20.5 %collective-permute-start.3 = (bf16[2,304,128]{2,1,0:T(8,128)(2,1)S(1)}, bf16[2,304,128]{2,1,0:T(8,128)(2,1)S(1)}, u32[]{:S(2)}, u32[]{:S(2)}) collective-permute-start(bf16[2,304,128]{2,1,0:T(8,128)(2,1)S(1)} %pad_maximum_fusion.1), channel_id=1, source_target_pairs={{0,14},{1,5},{2,0},{3,7},{4,2},{5,9},{6,4},{7,11},{8,6},{9,13},{10... | collective-permute-start | bytes 466952 | tf_op jit(solution)/shard_map/ppermute | solution.py:280
  29.1 18.5 %collective-permute-start.2 = (bf16[2,304,128]{2,1,0:T(8,128)(2,1)S(1)}, bf16[2,304,128]{2,1,0:T(8,128)(2,1)S(1)}, u32[]{:S(2)}, u32[]{:S(2)}) collective-permute-start(bf16[2,304,128]{2,1,0:T(8,128)(2,1)S(1)} %pad_maximum_fusion.1), channel_id=1, source_target_pairs={{0,2},{1,11},{2,4},{3,13},{4,6},{5,15},{6,8},{7,1},{8,10},{9,3},{1... | collective-permute-start | bytes 466952 | tf_op jit(solution)/shard_map/ppermute | solution.py:280
  34.1 13.5 %collective-permute-start.1 = (bf16[2,304,128]{2,1,0:T(8,128)(2,1)S(1)}, bf16[2,304,128]{2,1,0:T(8,128)(2,1)S(1)}, u32[]{:S(2)}, u32[]{:S(2)}) collective-permute-start(bf16[2,304,128]{2,1,0:T(8,128)(2,1)S(1)} %pad_maximum_fusion.1), channel_id=1, source_target_pairs={{0,8},{1,7},{2,10},{3,9},{4,12},{5,11},{6,14},{7,13},{8,0},{9,15},... | collective-permute-start | bytes 466952 | tf_op jit(solution)/shard_map/ppermute | solution.py:280
  36.2 0.9 copy-start
  37.1 12.9 %copy-start.8 = (s32[2,4]{1,0:T(2,128)S(1)}, s32[2,4]{1,0:T(2,128)}, u32[]{:S(2)}) copy-start(s32[2,4]{1,0:T(2,128)} %constant.65.clone) | copy-start | bytes 100
  38.3 23.8 %all-to-all-start.1 = ((bf16[32,16,304]{2,1,0:T(8,128)(2,1)}), bf16[32,16,304]{2,1,0:T(8,128)(2,1)S(1)}, u32[]{:S(2)}, u32[]{:S(2)}) async-start(bf16[32,16,304]{2,1,0:T(8,128)(2,1)} %shard_map.106), calls=%async_computation.1 | async-start | bytes 786432 | tf_op jit(solution)/shard_map/all_to_all | solution.py:284
  47.6 14.5 %copy-start.3 = (bf16[2,304,128]{2,1,0:T(8,128)(2,1)}, bf16[2,304,128]{2,1,0:T(8,128)(2,1)S(1)}, u32[]{:S(2)}) copy-start(bf16[2,304,128]{2,1,0:T(8,128)(2,1)S(1)} %collective-permute-done.4.q3_hbm) | copy-start | bytes 466948
  47.6 14.5 %copy-start.4 = (bf16[2,304,128]{2,1,0:T(8,128)(2,1)}, bf16[2,304,128]{2,1,0:T(8,128)(2,1)S(1)}, u32[]{:S(2)}) copy-start(bf16[2,304,128]{2,1,0:T(8,128)(2,1)S(1)} %collective-permute-done.3.q2_hbm) | copy-start | bytes 466948
  47.6 14.5 %copy-start.5 = (bf16[2,304,128]{2,1,0:T(8,128)(2,1)}, bf16[2,304,128]{2,1,0:T(8,128)(2,1)S(1)}, u32[]{:S(2)}) copy-start(bf16[2,304,128]{2,1,0:T(8,128)(2,1)S(1)} %collective-permute-done.2.q1_hbm) | copy-start | bytes 466948
  47.6 14.5 %copy-start.6 = (bf16[2,304,128]{2,1,0:T(8,128)(2,1)}, bf16[2,304,128]{2,1,0:T(8,128)(2,1)S(1)}, u32[]{:S(2)}) copy-start(bf16[2,304,128]{2,1,0:T(8,128)(2,1)S(1)} %collective-permute-done.1.q0_hbm) | copy-start | bytes 466948
  47.7 14.4 %collective-permute-start.5 = (bf16[8,304,128]{2,1,0:T(8,128)(2,1)S(1)}, bf16[8,304,128]{2,1,0:T(8,128)(2,1)S(1)}, u32[]{:S(2)}, u32[]{:S(2)}) collective-permute-start(bf16[8,304,128]{2,1,0:T(8,128)(2,1)S(1)} %pad_maximum_fusion), channel_id=1, source_target_pairs={{0,1},{1,0},{2,3},{3,2},{4,5},{5,4},{6,7},{7,6},{8,9},{9,8},{10,11... | collective-permute-start | bytes 1867784 | tf_op jit(solution)/shard_map/ppermute | solution.py:283
  62.1 0.7 copy-start.2
  62.1 0.9 copy-start.7
  76.1 7.7 %collective-permute-start.6 = (f32[8,304,128]{2,1,0:T(8,128)}, f32[8,304,128]{2,1,0:T(8,128)S(1)}, u32[]{:S(2)}, u32[]{:S(2)}) collective-permute-start(f32[8,304,128]{2,1,0:T(8,128)} %get-tuple-element.37), channel_id=1, source_target_pairs={{0,1},{1,0},{2,3},{3,2},{4,5},{5,4},{6,7},{7,6},{8,9},{9,8},{10,11... | collective-permute-start | bytes 3735560 | tf_op jit(solution)/shard_map/ppermute | solution.py:345
  79.7 21.4 %all-to-all-start.2 = ((bf16[32,16,304]{2,1,0:T(8,128)(2,1)}), bf16[32,16,304]{2,1,0:T(8,128)(2,1)S(1)}, u32[]{:S(2)}, u32[]{:S(2)}) async-start(bf16[32,16,304]{2,1,0:T(8,128)(2,1)} %get-tuple-element.39), calls=%async_computation.2 | async-start | bytes 786432 | tf_op jit(solution)/shard_map/all_to_all | solution.py:346
  85.2 15.9 %copy-start.1 = (f32[304,256]{1,0:T(8,128)S(1)}, f32[304,256]{1,0:T(8,128)}, u32[]{:S(2)}) copy-start(f32[304,256]{1,0:T(8,128)} %get-tuple-element.38.prim_ref) | copy-start | bytes 933892
  85.3 17.1 %collective-permute-start.10 = (bf16[2,304,128]{2,1,0:T(8,128)(2,1)S(1)}, bf16[2,304,128]{2,1,0:T(8,128)(2,1)S(1)}, u32[]{:S(2)}, u32[]{:S(2)}) collective-permute-start(bf16[2,304,128]{2,1,0:T(8,128)(2,1)S(1)} %get-tuple-element.44), channel_id=1, source_target_pairs={{0,0},{1,5},{2,2},{3,7},{4,4},{5,9},{6,6},{7,11},{8,8},{9,13},{10,... | collective-permute-start | bytes 466952 | tf_op jit(solution)/shard_map/ppermute | solution.py:348
  87.8 14.5 %collective-permute-start.9 = (bf16[2,304,128]{2,1,0:T(8,128)(2,1)S(1)}, bf16[2,304,128]{2,1,0:T(8,128)(2,1)S(1)}, u32[]{:S(2)}, u32[]{:S(2)}) collective-permute-start(bf16[2,304,128]{2,1,0:T(8,128)(2,1)S(1)} %get-tuple-element.45), channel_id=1, source_target_pairs={{0,2},{1,13},{2,4},{3,15},{4,6},{5,1},{6,8},{7,3},{8,10},{9,5},{10... | collective-permute-start | bytes 466952 | tf_op jit(solution)/shard_map/ppermute | solution.py:348
  92.8 12.7 %collective-permute-start.8 = (bf16[2,304,128]{2,1,0:T(8,128)(2,1)S(1)}, bf16[2,304,128]{2,1,0:T(8,128)(2,1)S(1)}, u32[]{:S(2)}, u32[]{:S(2)}) collective-permute-start(bf16[2,304,128]{2,1,0:T(8,128)(2,1)S(1)} %get-tuple-element.46), channel_id=1, source_target_pairs={{0,14},{1,7},{2,0},{3,9},{4,2},{5,11},{6,4},{7,13},{8,6},{9,15},{1... | collective-permute-start | bytes 466952 | tf_op jit(solution)/shard_map/ppermute | solution.py:348
  95.3 13.0 %collective-permute-start.7 = (bf16[2,304,128]{2,1,0:T(8,128)(2,1)S(1)}, bf16[2,304,128]{2,1,0:T(8,128)(2,1)S(1)}, u32[]{:S(2)}, u32[]{:S(2)}) collective-permute-start(bf16[2,304,128]{2,1,0:T(8,128)(2,1)S(1)} %get-tuple-element.47), channel_id=1, source_target_pairs={{0,8},{1,11},{2,10},{3,13},{4,12},{5,15},{6,14},{7,1},{8,0},{9,3},... | collective-permute-start | bytes 466952 | tf_op jit(solution)/shard_map/ppermute | solution.py:348
  108.4 3.3 %collective-permute-start.11 = (f32[304,128]{1,0:T(8,128)S(1)}, f32[304,128]{1,0:T(8,128)S(1)}, u32[]{:S(2)}, u32[]{:S(2)}) collective-permute-start(f32[304,128]{1,0:T(8,128)S(1)} %get-tuple-element.49), channel_id=1, source_target_pairs={{0,1},{1,0},{2,3},{3,2},{4,5},{5,4},{6,7},{7,6},{8,9},{9,8},{10,11... | collective-permute-start | bytes 466952 | tf_op jit(solution)/shard_map/ppermute | solution.py:352

commit v3 on v2

--- a/solution.py
+++ b/solution.py
@@ -11,13 +11,15 @@
 LANES = 128
 CAP = 16
 ROW_CHUNK = 32
+STEP = 8
+FEW = 4
 BIG = 60
 
 VMEM = pl.BlockSpec(memory_space=pltpu.VMEM)
 SMEM = pl.BlockSpec(memory_space=pltpu.SMEM)
 ANY = pl.BlockSpec(memory_space=pl.ANY)
 
-HOPS = ((4, 1, 7, 0), (3, 5, 2, 6))
+HOPS = ((0, 7, 1, 4), (6, 2, 5, 3))
 
 
 def iota(shape, dim):
@@ -79,17 +81,16 @@
     return hot, jnp.sum(jnp.where(hot, before, 0.0), axis=0, keepdims=True)
 
 
-def pad_kernel(qt_hbm, wt_hbm, qp_ref, wp_ref, qt_ref, wt_ref, sems):
-    copies = fetch(sems, (qt_hbm, qt_ref), (wt_hbm, wt_ref))
+def start_kernel(
+    owner_hbm, row_hbm, qt_hbm, wt_hbm, ask_ref, qp_ref, wp_ref, owner_ref, row_ref, qt_ref, wt_ref, sems
+):
+    copies = fetch(sems, (owner_hbm, owner_ref), (row_hbm, row_ref), (qt_hbm, qt_ref), (wt_hbm, wt_ref))
     dim = qt_hbm.shape[0]
-    for copy, src, dst in zip(copies, (qt_ref, wt_ref), (qp_ref, wp_ref)):
-        copy.wait()
-        dst[:dim, :] = src[...]
+    for dst in (qp_ref, wp_ref):
         dst[dim:, :] = jnp.zeros((dst.shape[0] - dim, dst.shape[1]), dst.dtype)
-
-
-def ask_kernel(owner_hbm, row_hbm, ask_ref, owner_ref, row_ref, sems):
-    wait(fetch(sems, (owner_hbm, owner_ref), (row_hbm, row_ref)))
+    wait(copies)
+    qp_ref[:dim, :] = qt_ref[...]
+    wp_ref[:dim, :] = wt_ref[...]
     sections = ask_ref.shape[0]
     owner = owner_ref[...]
     hot, rank = ranks(owner, sections)
@@ -115,8 +116,8 @@
 
 
 def prepare_kernel(
-    first_ref, prop_ref, owner_ref, row_ref, wt_ref, bucket_ref, weight_ref,
-    comp_ref, comp_t_ref, slots_ref, wrow_ref, value_ref,
+    first_ref, prop_ref, owner_ref, row_ref, wt_ref, label_ref, bucket_ref, weight_ref,
+    comp_ref, comp_t_ref, slots_ref, wrow_ref, key_ref, value_ref, count_ref,
 ):
     sections = comp_ref.shape[1] // CAP
     owner = owner_ref[...]
@@ -142,34 +143,54 @@
     value = jnp.zeros(bucket.shape, F32)
     for b in range(prop_ref.shape[0]):
         value = jnp.where(bucket == b, prop_ref[b], value)
-    value_ref[...] = value * weight_ref[...] * 0.5
+    value = value * weight_ref[...] * 0.5
+    positives = label_ref[...]
+    shift = prim.bit_length() - 1
+    leaf_mask = stride // prim - 1
+    here = jnp.where((positives >> shift) & leaf_mask == leaf_base >> shift, 1, 0)
+    places = positives.shape[0]
+    keys = [jnp.full((1, positives.shape[1]), -1, I32)] * places
+    values = [jnp.zeros((1, positives.shape[1]), F32)] * places
+    count = jnp.zeros((1, positives.shape[1]), I32)
+    for p in range(places):
+        at = jnp.where(here[p:p + 1] == 1, count, places)
+        for k in range(p + 1):
+            keys[k] = jnp.where(at == k, positives[p:p + 1], keys[k])
+            values[k] = jnp.where(at == k, value[p:p + 1], values[k])
+        count = count + here[p:p + 1]
+    for k in range(places):
+        key_ref[k:k + 1, :] = keys[k]
+        value_ref[k:k + 1, :] = values[k]
+    for b in range(count_ref.shape[0]):
+        count_ref[b] = jnp.max(count[:, b * LANES:(b + 1) * LANES].astype(F32)).astype(I32)
 
 
 def grad_kernel(
-    columns_ref, arrived_hbm, q0_hbm, q1_hbm, q2_hbm, q3_hbm, sib_hbm,
+    columns_ref, count_ref, arrived_hbm, q0_hbm, q1_hbm, q2_hbm, q3_hbm, sib_hbm,
     comp_hbm, comp_t_hbm, slots_hbm, wrow_hbm, wt_hbm, label_hbm, value_hbm, weight_hbm,
     part_sib_hbm, part_own_hbm, prim_hbm, back_ref,
-    arrived_ref, sib_ref, own_ref, comp_ref, comp_t_ref, slots_ref, w_scr, wt_scr, label_ref, value_ref, weight_ref,
+    arrived_ref, q_ref, comp_ref, comp_t_ref, slots_ref, w_scr, wt_scr, label_ref, value_ref, weight_ref,
     part_ref, prim_ref, logit_scr, coef_scr, copy_scr, in_sems, out_sems,
 ):
     prim = wt_hbm.shape[1]
     slots = slots_ref.shape[0]
     dim = wt_hbm.shape[0]
+    half = sib_hbm.shape[0]
     copies = fetch(
         in_sems,
         (arrived_hbm, arrived_ref),
         (comp_hbm, comp_ref),
         (wrow_hbm, w_scr.at[:prim, :]),
         (wt_hbm, wt_scr.at[:, :prim]),
-        (sib_hbm, sib_ref),
+        (sib_hbm, q_ref.at[:half]),
         (slots_hbm, slots_ref),
         (label_hbm, label_ref),
         (value_hbm, value_ref),
         (weight_hbm, weight_ref),
-        (q0_hbm, own_ref.at[0:2]),
-        (q1_hbm, own_ref.at[2:4]),
-        (q2_hbm, own_ref.at[4:6]),
-        (q3_hbm, own_ref.at[6:8]),
+        (q0_hbm, q_ref.at[half + 0:half + 2]),
+        (q1_hbm, q_ref.at[half + 2:half + 4]),
+        (q2_hbm, q_ref.at[half + 4:half + 6]),
+        (q3_hbm, q_ref.at[half + 6:half + 8]),
         (comp_t_hbm, comp_t_ref),
     )
     prim_ref[...] = jnp.zeros(prim_ref.shape, F32)
@@ -180,54 +201,62 @@
     wt_scr[:, prim:] = fetched.T.astype(BF16)
     wait(copies[2:])
 
-    def pair(q, k):
+    def fill(side, column, depth):
+        at = pl.ds(pl.multiple_of(column * LANES, LANES), LANES)
+        half_weight = weight_ref[:, at] * 0.5
+        labels = label_ref[:, at]
+        values = value_ref[:, at]
+        lanes = slice(side * LANES, (side + 1) * LANES)
+        for r in range(0, slots, ROW_CHUNK):
+            rows = slice(r, r + ROW_CHUNK)
+            t = jnp.tanh(logit_scr[rows, lanes])
+            slot = slots_ref[rows, :]
+            total = jnp.where(slot == labels[0:1, :], values[0:1, :], 0.0)
+            for p in range(1, depth):
+                total = total + jnp.where(slot == labels[p:p + 1, :], values[p:p + 1, :], 0.0)
+            hit = total > 0.0
+            scale = jnp.where(hit, total, half_weight)
+            coef_scr[rows, lanes] = (scale * (t + jnp.where(hit, -1.0, 1.0))).astype(BF16)
+
+    def step(k, carry):
+        first = k * STEP
+        q = jnp.concatenate([q_ref[first + i] for i in range(STEP)], axis=1)
         logit_scr[...] = nn(w_scr[...], q)
-        for side in range(2):
-            at = pl.ds(pl.multiple_of(columns_ref[2 * k + side] * LANES, LANES), LANES)
-            half_weight = weight_ref[:, at] * 0.5
-            labels = label_ref[:, at]
-            values = value_ref[:, at]
-            lanes = slice(side * LANES, (side + 1) * LANES)
-            for r in range(0, slots, ROW_CHUNK):
-                rows = slice(r, r + ROW_CHUNK)
-                t = jnp.tanh(logit_scr[rows, lanes])
-                slot = slots_ref[rows, :]
-                total = jnp.where(slot == labels[0:1, :], values[0:1, :], 0.0)
-                for p in range(1, labels.shape[0]):
-                    total = total + jnp.where(slot == labels[p:p + 1, :], values[p:p + 1, :], 0.0)
-                hit = total > 0.0
-                scale = jnp.where(hit, total, half_weight)
-                coef_scr[rows, lanes] = (scale * (t + jnp.where(hit, -1.0, 1.0))).astype(BF16)
+        for side in range(STEP):
+            column = columns_ref[first + side]
+            few = count_ref[column] <= FEW
+            pl.when(few)(lambda: fill(side, column, FEW))
+            pl.when(jnp.logical_not(few))(lambda: fill(side, column, label_ref.shape[0]))
         coef = coef_scr[...]
+        part = nn(wt_scr[...], coef)
+        for i in range(STEP):
+            part_ref[first + i] = part[:, i * LANES:(i + 1) * LANES]
+        source = part_ref.at[pl.ds(first, STEP)]
+
+        @pl.when(first < half)
+        def _():
+            pltpu.make_async_copy(source, part_sib_hbm.at[pl.ds(first, STEP)], out_sems.at[k]).start()
+
+        @pl.when(first >= half)
+        def _():
+            pltpu.make_async_copy(source, part_own_hbm.at[pl.ds(first - half, STEP)], out_sems.at[k]).start()
+
         prim_ref[...] += nt(q, coef[:prim])
         copy_scr[...] += nt(coef[prim:], q)
-        return nn(wt_scr[...], coef)
-
-    chips = sib_ref.shape[0] // 2
-
-    def step(k, carry):
-        sib = k < chips
-        at = 2 * jnp.where(sib, k, k - chips)
-
-        def run(q_ref, out_hbm):
-            part = pair(jnp.concatenate([q_ref[at], q_ref[at + 1]], axis=1), jnp.where(sib, k + chips, k - chips))
-            part_ref[2 * k] = part[:, :LANES]
-            part_ref[2 * k + 1] = part[:, LANES:]
-            pltpu.make_async_copy(part_ref.at[pl.ds(2 * k, 2)], out_hbm.at[pl.ds(at, 2)], out_sems.at[k]).start()
-
-        pl.when(sib)(lambda: run(sib_ref, part_sib_hbm))
-        pl.when(jnp.logical_not(sib))(lambda: run(own_ref, part_own_hbm))
         return carry
 
-    lax.fori_loop(0, 2 * chips, step, 0)
-    last = pltpu.make_async_copy(prim_ref, prim_hbm, out_sems.at[2 * chips])
+    steps = 2 * half // STEP
+    lax.fori_loop(0, steps, step, 0)
+    last = pltpu.make_async_copy(prim_ref, prim_hbm, out_sems.at[steps])
     last.start()
     back = nn(comp_t_ref[...], copy_scr[...].astype(BF16))
     back_ref[...] = back.astype(BF16).reshape(back_ref.shape)
-    for k in range(2 * chips):
-        out_hbm = part_sib_hbm if k < chips else part_own_hbm
-        at = 2 * (k % chips)
-        pltpu.make_async_copy(part_ref.at[2 * k:2 * k + 2], out_hbm.at[at:at + 2], out_sems.at[k]).wait()
+    for k in range(steps):
+        first = k * STEP
+        out_hbm, at = (part_sib_hbm, first) if first < half else (part_own_hbm, first - half)
+        pltpu.make_async_copy(
+            part_ref.at[first:first + STEP], out_hbm.at[at:at + STEP], out_sems.at[k]
+        ).wait()
     last.wait()
 
 
@@ -257,25 +286,20 @@
     row = copy_row.reshape(1, n)
     dim = 16 * pl.cdiv(features, 16)
 
-    ask = call(
-        ask_kernel,
-        shape((sections, 8, LANES), F32),
-        [ANY] * 2,
-        scratch=(pltpu.VMEM((1, n), I32), pltpu.VMEM((1, n), I32), pltpu.SemaphoreType.DMA((2,))),
-        vmem=BIG,
-    )(owner, row)
-    wanted = lax.all_to_all(ask, "section", split_axis=0, concat_axis=0, tiled=True)
-    qp, wp = call(
-        pad_kernel,
-        (shape((dim, queries), BF16), shape((dim, prim), BF16)),
-        [ANY] * 2,
+    ask, qp, wp = call(
+        start_kernel,
+        (shape((sections, 8, LANES), F32), shape((dim, queries), BF16), shape((dim, prim), BF16)),
+        [ANY] * 4,
         scratch=(
+            pltpu.VMEM((1, n), I32),
+            pltpu.VMEM((1, n), I32),
             pltpu.VMEM((features, queries), BF16),
             pltpu.VMEM((features, prim), BF16),
-            pltpu.SemaphoreType.DMA((2,)),
+            pltpu.SemaphoreType.DMA((4,)),
         ),
         vmem=BIG,
-    )(*after((query_feats.T, primary_w.T), ask))
+    )(owner, row, query_feats.T, primary_w.T)
+    wanted = lax.all_to_all(ask, "section", split_axis=0, concat_axis=0, tiled=True)
     both = jnp.stack([qp, lax.ppermute(qp, "leaf", sibling)])
     own = [lax.ppermute(both, "leaf", hops(chips, k, 1)) for k in range(4)]
     served = call(serve_kernel, shape((sections, CAP, dim), BF16), [VMEM] * 2)(wanted, wp)
@@ -286,18 +310,21 @@
     first = (section_id * leaves + leaf_id) * prim
     numbers = jnp.stack([first, leaf_id * prim, jnp.int32(leaves * prim)]).astype(I32)
     weight = query_weight.reshape(1, -1)
-    comp, comp_t, slot_ids, wrow, value = call(
+    comp, comp_t, slot_ids, wrow, key, value, count = call(
         prepare_kernel,
         (
             shape((n, sections * CAP), BF16),
             shape((sections * CAP, n), BF16),
             shape((slots, LANES), I32),
             shape((prim, dim), BF16),
+            shape(positive_label.shape[::-1], I32),
             shape(positive_label.shape[::-1], F32),
+            shape((leaves,), I32),
         ),
-        [SMEM, SMEM] + [VMEM] * 5,
+        [SMEM, SMEM] + [VMEM] * 6,
         vmem=BIG,
-    )(numbers, inv_prop, owner, row, wp, positive_bucket.T, weight)
+        outs=(VMEM,) * 6 + (SMEM,),
+    )(numbers, inv_prop, owner, row, wp, positive_label.T, positive_bucket.T, weight)
 
     core = leaf_id % 2
     chip = leaf_id // 2
@@ -306,7 +333,7 @@
     other = (chip - near[1 - core]) % chips
     ends = jnp.stack([core, 1 - core])
     columns = jnp.concatenate(
-        [(2 * mine[:, None] + ends[None, :]).reshape(-1), (2 * other[:, None] + ends[None, ::-1]).reshape(-1)]
+        [(2 * other[:, None] + ends[None, ::-1]).reshape(-1), (2 * mine[:, None] + ends[None, :]).reshape(-1)]
     ).astype(I32)
     total = positive_label.shape[0]
     part_sib, part_own, prim_t, back = call(
@@ -317,11 +344,10 @@
             shape((dim, prim), F32),
             shape((sections, CAP, dim), BF16),
         ),
-        [SMEM] + [ANY] * 14,
+        [SMEM] * 2 + [ANY] * 14,
         scratch=(
             pltpu.VMEM(arrived.shape, BF16),
-            pltpu.VMEM(sib.shape, BF16),
-            pltpu.VMEM(sib.shape, BF16),
+            pltpu.VMEM((leaves, dim, queries), BF16),
             pltpu.VMEM(comp.shape, BF16),
             pltpu.VMEM(comp_t.shape, BF16),
             pltpu.VMEM((slots, LANES), I32),
@@ -332,15 +358,15 @@
             pltpu.VMEM((1, total), F32),
             pltpu.VMEM((leaves, dim, queries), F32),
             pltpu.VMEM((dim, prim), F32),
-            pltpu.VMEM((slots, 2 * LANES), F32),
-            pltpu.VMEM((slots, 2 * LANES), BF16),
+            pltpu.VMEM((slots, STEP * LANES), F32),
+            pltpu.VMEM((slots, STEP * LANES), BF16),
             pltpu.VMEM((n, dim), F32),
             pltpu.SemaphoreType.DMA((14,)),
-            pltpu.SemaphoreType.DMA((chips + 1,)),
+            pltpu.SemaphoreType.DMA((leaves // STEP + 1,)),
         ),
         vmem=BIG,
         outs=(ANY, ANY, ANY, VMEM),
-    )(columns, arrived, *own, sib, comp, comp_t, slot_ids, wrow, wp, positive_label.T, value, weight)
+    )(columns, count, arrived, *own, sib, comp, comp_t, slot_ids, wrow, wp, key, value, weight)
 
     swapped = lax.ppermute(part_sib, "leaf", sibling)
     returned = lax.all_to_all(back, "section", split_axis=0, concat_axis=0, tiled=True)

time: 113 us -> 106 us (0.938)
  Pallas kernels: 21 us -> 17.2 us
  waiting for transfers between devices: 15.7 us -> 13.6 us
    pallas_call x1, Pallas kernels: 13 us -> 9.98 us  [on_device(): call(grad_kernel, (shape((chips, dim, queries), F32), shape((chips, dim,...]
    ppermute x4, starting transfers between devices: 15.8 us -> 13.4 us  [on_device(): lax.ppermute(sums[2 * k:2 * k + 2], 'leaf', hops(chips, k, -1))]
    pallas_call x2 -> x1, Pallas kernels: 3.35 us -> 2 us  [on_device(): call(start_kernel, (shape((sections, 8, LANES), F32), shape((dim, queries...]
    ppermute x4, waiting for transfers between devices: 5.97 us -> 4.65 us  [on_device(): lax.ppermute(sums[2 * k:2 * k + 2], 'leaf', hops(chips, k, -1))]
    ppermute x4, starting transfers between devices: 14.9 us -> 16.1 us  [on_device(): own = [lax.ppermute(both, 'leaf', hops(chips, k, 1)) for k in range(4)]]
  transfers between devices with their start and end apart: 15 -> 15, of which waited for: 4 -> 5; matrix products, arithmetic and copies ran while one was open for 4% -> 4% of each run, Pallas kernels for 4% -> 5%
where the time goes in v3:
time: 106 us; the launch traced here: 105 us
  starting transfers between devices  66.9 us (63%)
  Pallas kernels  17.2 us (16%)
  waiting for transfers between devices  13.6 us (13%)
  other arithmetic  4.63 us (4%)
  local copies, waits for them, and re-layouts  2.17 us (2%)
    ppermute x4, starting transfers between devices, on_device(): own = [lax.ppermute(both, 'leaf', hops(chips, k, 1)) for k in range(4)]  16.1 us
    ppermute x4, starting transfers between devices, on_device(): lax.ppermute(sums[2 * k:2 * k + 2], 'leaf', hops(chips, k, -1))  13.4 us
    pallas_call x1, Pallas kernels, on_device(): call(grad_kernel, (shape((chips, dim, queries), F32), shape((chips, dim,...  9.98 us
    all_to_all x1, starting transfers between devices, on_device(): lax.all_to_all(served, 'section', split_axis=0, concat_axis=0, tiled=True)  9.21 us
    ppermute x1, starting transfers between devices, on_device(): both = jnp.stack([qp, lax.ppermute(qp, 'leaf', sibling)])  8.79 us
    all_to_all x1, waiting for transfers between devices, on_device(): lax.all_to_all(served, 'section', split_axis=0, concat_axis=0, tiled=True)  7.73 us
    all_to_all x1, starting transfers between devices, on_device(): lax.all_to_all(ask, 'section', split_axis=0, concat_axis=0, tiled=True)  7.52 us
    ppermute x4, waiting for transfers between devices, on_device(): lax.ppermute(sums[2 * k:2 * k + 2], 'leaf', hops(chips, k, -1))  4.65 us
  transfers between devices with their start and end apart: 15, of which 5 were waited for; matrix products, arithmetic and copies ran while one was open for 4% of the time, Pallas kernels for 5%

profile of v3, /device:TPU:1, one launch (start us, length us, event | category | flops | bytes accessed | tf_op | source)
XLA Modules:
  0.0 105.4 jit_solution(12902521669138432218)
XLA Ops:
  0.6 2.0 %shard_map.104 = (f32[32,8,128]{2,1,0:T(8,128)}, bf16[304,128]{1,0:T(8,128)(2,1)}, bf16[304,256]{1,0:T(8,128)(2,1)}) custom-call(s32[1,256]{1,0:T(1,128)} %bitcast.33, s32[1,256]{1,0:T(1,128)} %bitcast.35, bf16[300,128]{1,0:T(8,128)(2,1)} %bitcast.26, bf16[300,256]{1,0:T(8,128)(2,1)} %bitcast.25), custom_call_target="tpu_custom_call" | custom-call | tf_op jit(solution)/shard_map/pallas_call | solution.py:289
  2.6 8.8 %collective-permute-start = (bf16[304,128]{1,0:T(8,128)(2,1)}, bf16[304,128]{1,0:T(8,128)(2,1)S(1)}, u32[]{:S(2)}, u32[]{:S(2)}) collective-permute-start(bf16[304,128]{1,0:T(8,128)(2,1)} %get-tuple-element.27), channel_id=1, source_target_pairs={{0,1},{1,0},{2,3},{3,2},{4,5},{5,4},{6,7},{7,6},{8,9},{9,8},{10,11... | collective-permute-start | bytes 233480 | tf_op jit(solution)/shard_map/ppermute | solution.py:303
  11.4 7.5 %all-to-all-start = ((f32[32,8,128]{2,1,0:T(8,128)}), f32[32,8,128]{2,1,0:T(8,128)S(1)}, u32[]{:S(2)}, u32[]{:S(2)}) async-start(f32[32,8,128]{2,1,0:T(8,128)} %get-tuple-element.26), calls=%async_computation | async-start | bytes 262144 | tf_op jit(solution)/shard_map/all_to_all | solution.py:302
  19.9 5.2 %collective-permute-start.4 = (bf16[2,304,128]{2,1,0:T(8,128)(2,1)S(1)}, bf16[2,304,128]{2,1,0:T(8,128)(2,1)S(1)}, u32[]{:S(2)}, u32[]{:S(2)}) collective-permute-start(bf16[2,304,128]{2,1,0:T(8,128)(2,1)S(1)} %pad_maximum_fusion.1), channel_id=1, source_target_pairs={{0,8},{1,7},{2,10},{3,9},{4,12},{5,11},{6,14},{7,13},{8,0},{9,15},... | collective-permute-start | bytes 466952 | tf_op jit(solution)/shard_map/ppermute | solution.py:304
  25.1 3.4 %collective-permute-start.3 = (bf16[2,304,128]{2,1,0:T(8,128)(2,1)S(1)}, bf16[2,304,128]{2,1,0:T(8,128)(2,1)S(1)}, u32[]{:S(2)}, u32[]{:S(2)}) collective-permute-start(bf16[2,304,128]{2,1,0:T(8,128)(2,1)S(1)} %pad_maximum_fusion.1), channel_id=1, source_target_pairs={{0,2},{1,11},{2,4},{3,13},{4,6},{5,15},{6,8},{7,1},{8,10},{9,3},{1... | collective-permute-start | bytes 466952 | tf_op jit(solution)/shard_map/ppermute | solution.py:304
  28.5 3.9 %collective-permute-start.2 = (bf16[2,304,128]{2,1,0:T(8,128)(2,1)S(1)}, bf16[2,304,128]{2,1,0:T(8,128)(2,1)S(1)}, u32[]{:S(2)}, u32[]{:S(2)}) collective-permute-start(bf16[2,304,128]{2,1,0:T(8,128)(2,1)S(1)} %pad_maximum_fusion.1), channel_id=1, source_target_pairs={{0,14},{1,5},{2,0},{3,7},{4,2},{5,9},{6,4},{7,11},{8,6},{9,13},{10... | collective-permute-start | bytes 466952 | tf_op jit(solution)/shard_map/ppermute | solution.py:304
  32.4 3.6 %collective-permute-start.1 = (bf16[2,304,128]{2,1,0:T(8,128)(2,1)S(1)}, bf16[2,304,128]{2,1,0:T(8,128)(2,1)S(1)}, u32[]{:S(2)}, u32[]{:S(2)}) collective-permute-start(bf16[2,304,128]{2,1,0:T(8,128)(2,1)S(1)} %pad_maximum_fusion.1), channel_id=1, source_target_pairs={{0,0},{1,13},{2,2},{3,15},{4,4},{5,1},{6,6},{7,3},{8,8},{9,5},{10,... | collective-permute-start | bytes 466952 | tf_op jit(solution)/shard_map/ppermute | solution.py:304
  37.0 1.2 %shard_map.106 = bf16[32,16,304]{2,1,0:T(8,128)(2,1)} custom-call(f32[32,8,128]{2,1,0:T(8,128)S(1)} %all-to-all-done.ask_ref, bf16[304,256]{1,0:T(8,128)(2,1)S(1)} %copy-done), custom_call_target="tpu_custom_call" | custom-call | tf_op jit(solution)/shard_map/pallas_call | solution.py:305
  38.2 9.2 %all-to-all-start.1 = ((bf16[32,16,304]{2,1,0:T(8,128)(2,1)}), bf16[32,16,304]{2,1,0:T(8,128)(2,1)S(1)}, u32[]{:S(2)}, u32[]{:S(2)}) async-start(bf16[32,16,304]{2,1,0:T(8,128)(2,1)} %shard_map.106), calls=%async_computation.1 | async-start | bytes 786432 | tf_op jit(solution)/shard_map/all_to_all | solution.py:308
  47.6 2.1 %collective-permute-start.5 = (bf16[8,304,128]{2,1,0:T(8,128)(2,1)S(1)}, bf16[8,304,128]{2,1,0:T(8,128)(2,1)S(1)}, u32[]{:S(2)}, u32[]{:S(2)}) collective-permute-start(bf16[8,304,128]{2,1,0:T(8,128)(2,1)S(1)} %pad_maximum_fusion), channel_id=1, source_target_pairs={{0,1},{1,0},{2,3},{3,2},{4,5},{5,4},{6,7},{7,6},{8,9},{9,8},{10,11... | collective-permute-start | bytes 1867784 | tf_op jit(solution)/shard_map/ppermute | solution.py:307
  50.8 2.7 %shard_map.105 = (bf16[256,512]{1,0:T(8,128)(2,1)}, bf16[512,256]{1,0:T(8,128)(2,1)}, s32[512,128]{1,0:T(8,128)}, bf16[256,304]{1,0:T(8,128)(2,1)}, s32[8,2048]{...) custom-call(s32[3]{0:T(128)} %pad_add_fusion.2.first_ref, f32[16]{0:T(128)} %prop_ref.1, s32[1,256]{1,0:T(1,128)} %bitcast.34, ...), custom_call_target="tpu_custom_call" | custom-call | tf_op jit(solution)/shard_map/pallas_call | solution.py:313
  54.2 7.7 %all-to-all-done.1.arrived_hbm = bf16[32,16,304]{2,1,0:T(8,128)(2,1)S(1)} async-done(((bf16[32,16,304]{2,1,0:T(8,128)(2,1)}), bf16[32,16,304]{2,1,0:T(8,128)(2,1)S(1)}, u32[]{:S(2)}, u32[]{:S(2)}) %all-to-all-start.1) | async-done | bytes 311328 | tf_op jit(solution)/shard_map/all_to_all | solution.py:308
  62.9 10.0 %shard_map.107 = (f32[8,304,128]{2,1,0:T(8,128)}, f32[8,304,128]{2,1,0:T(8,128)}, f32[304,256]{1,0:T(8,128)}, bf16[32,16,304]{2,1,0:T(8,128)(2,1)}) custom-call(s32[16]{0:T(128)} %pad_add_fusion.1.columns_ref, s32[16]{0:T(128)} %get-tuple-element.25.count_ref, bf16[32,16,304]{2,1,0:T(8,128)(2,1)} %copy-done.2, bf16[2,304,128]{2,1,0:T(8,128)(2,1)} %copy-done.7, ...), custom_call_target="tpu_custom_call" | custom-call | tf_op jit(solution)/shard_map/pallas_call | solution.py:339
  72.9 3.6 %collective-permute-start.6 = (f32[8,304,128]{2,1,0:T(8,128)}, f32[8,304,128]{2,1,0:T(8,128)S(1)}, u32[]{:S(2)}, u32[]{:S(2)}) collective-permute-start(f32[8,304,128]{2,1,0:T(8,128)} %get-tuple-element.39), channel_id=1, source_target_pairs={{0,1},{1,0},{2,3},{3,2},{4,5},{5,4},{6,7},{7,6},{8,9},{9,8},{10,11... | collective-permute-start | bytes 3735560 | tf_op jit(solution)/shard_map/ppermute | solution.py:371
  76.5 4.0 %all-to-all-start.2 = ((bf16[32,16,304]{2,1,0:T(8,128)(2,1)}), bf16[32,16,304]{2,1,0:T(8,128)(2,1)S(1)}, u32[]{:S(2)}, u32[]{:S(2)}) async-start(bf16[32,16,304]{2,1,0:T(8,128)(2,1)} %get-tuple-element.41), calls=%async_computation.2 | async-start | bytes 786432 | tf_op jit(solution)/shard_map/all_to_all | solution.py:372
  80.6 1.4 %add_convert_fusion = bf16[8,304,128]{2,1,0:T(8,128)(2,1)S(1)} fusion(f32[8,304,128]{2,1,0:T(8,128)} %get-tuple-element.38, f32[8,304,128]{2,1,0:T(8,128)S(1)} %collective-permute-done.6), kind=kLoop, calls=%fused_computation | loop fusion | flops 622592 | bytes 3112960 | tf_op jit(solution)/shard_map/convert_element_type | solution.py:373
  82.0 2.4 %collective-permute-start.10 = (bf16[2,304,128]{2,1,0:T(8,128)(2,1)S(1)}, bf16[2,304,128]{2,1,0:T(8,128)(2,1)S(1)}, u32[]{:S(2)}, u32[]{:S(2)}) collective-permute-start(bf16[2,304,128]{2,1,0:T(8,128)(2,1)S(1)} %get-tuple-element.46), channel_id=1, source_target_pairs={{0,8},{1,11},{2,10},{3,13},{4,12},{5,15},{6,14},{7,1},{8,0},{9,3},... | collective-permute-start | bytes 466952 | tf_op jit(solution)/shard_map/ppermute | solution.py:374
  84.5 4.8 %collective-permute-start.9 = (bf16[2,304,128]{2,1,0:T(8,128)(2,1)S(1)}, bf16[2,304,128]{2,1,0:T(8,128)(2,1)S(1)}, u32[]{:S(2)}, u32[]{:S(2)}) collective-permute-start(bf16[2,304,128]{2,1,0:T(8,128)(2,1)S(1)} %get-tuple-element.47), channel_id=1, source_target_pairs={{0,14},{1,7},{2,0},{3,9},{4,2},{5,11},{6,4},{7,13},{8,6},{9,15},{1... | collective-permute-start | bytes 466952 | tf_op jit(solution)/shard_map/ppermute | solution.py:374
  89.3 2.0 %collective-permute-start.8 = (bf16[2,304,128]{2,1,0:T(8,128)(2,1)S(1)}, bf16[2,304,128]{2,1,0:T(8,128)(2,1)S(1)}, u32[]{:S(2)}, u32[]{:S(2)}) collective-permute-start(bf16[2,304,128]{2,1,0:T(8,128)(2,1)S(1)} %get-tuple-element.48), channel_id=1, source_target_pairs={{0,2},{1,13},{2,4},{3,15},{4,6},{5,1},{6,8},{7,3},{8,10},{9,5},{10... | collective-permute-start | bytes 466952 | tf_op jit(solution)/shard_map/ppermute | solution.py:374
  91.2 4.2 %collective-permute-start.7 = (bf16[2,304,128]{2,1,0:T(8,128)(2,1)S(1)}, bf16[2,304,128]{2,1,0:T(8,128)(2,1)S(1)}, u32[]{:S(2)}, u32[]{:S(2)}) collective-permute-start(bf16[2,304,128]{2,1,0:T(8,128)(2,1)S(1)} %get-tuple-element.49), channel_id=1, source_target_pairs={{0,0},{1,5},{2,2},{3,7},{4,4},{5,9},{6,6},{7,11},{8,8},{9,13},{10,... | collective-permute-start | bytes 466952 | tf_op jit(solution)/shard_map/ppermute | solution.py:374
  95.5 1.2 %shard_map.108 = f32[300,256]{1,0:T(8,128)} custom-call(f32[32,8,128]{2,1,0:T(8,128)S(1)} %all-to-all-done.ask_ref, f32[304,256]{1,0:T(8,128)S(1)} %copy-done.1, bf16[32,16,304]{2,1,0:T(8,128)(2,1)S(1)} %all-to-all-done.2.returned_ref), custom_call_target="tpu_custom_call" | custom-call | tf_op jit(solution)/shard_map/pallas_call | solution.py:375
  96.7 2.0 %collective-permute-done.9 = bf16[2,304,128]{2,1,0:T(8,128)(2,1)S(1)} collective-permute-done((bf16[2,304,128]{2,1,0:T(8,128)(2,1)S(1)}, bf16[2,304,128]{2,1,0:T(8,128)(2,1)S(1)}, u32[]{:S(2)}, u32[]{:S(2)}) %collective-permute-start.9) | collective-permute-done | bytes 155680 | tf_op jit(solution)/shard_map/ppermute | solution.py:374
  98.7 1.4 %collective-permute-done.8 = bf16[2,304,128]{2,1,0:T(8,128)(2,1)S(1)} collective-permute-done((bf16[2,304,128]{2,1,0:T(8,128)(2,1)S(1)}, bf16[2,304,128]{2,1,0:T(8,128)(2,1)S(1)}, u32[]{:S(2)}, u32[]{:S(2)}) %collective-permute-start.8) | collective-permute-done | bytes 155680 | tf_op jit(solution)/shard_map/ppermute | solution.py:374
  101.5 2.1 %collective-permute-start.11 = (f32[304,128]{1,0:T(8,128)S(1)}, f32[304,128]{1,0:T(8,128)S(1)}, u32[]{:S(2)}, u32[]{:S(2)}) collective-permute-start(f32[304,128]{1,0:T(8,128)S(1)} %get-tuple-element.51), channel_id=1, source_target_pairs={{0,1},{1,0},{2,3},{3,2},{4,5},{5,4},{6,7},{7,6},{8,9},{9,8},{10,11... | collective-permute-start | bytes 466952 | tf_op jit(solution)/shard_map/ppermute | solution.py:378
  (44 shorter events, 7.8 us)
Async XLA Ops:
  2.6 16.3 %collective-permute-start = (bf16[304,128]{1,0:T(8,128)(2,1)}, bf16[304,128]{1,0:T(8,128)(2,1)S(1)}, u32[]{:S(2)}, u32[]{:S(2)}) collective-permute-start(bf16[304,128]{1,0:T(8,128)(2,1)} %get-tuple-element.27), channel_id=1, source_target_pairs={{0,1},{1,0},{2,3},{3,2},{4,5},{5,4},{6,7},{7,6},{8,9},{9,8},{10,11... | collective-permute-start | bytes 233480 | tf_op jit(solution)/shard_map/ppermute | solution.py:303
  11.4 24.6 %all-to-all-start = ((f32[32,8,128]{2,1,0:T(8,128)}), f32[32,8,128]{2,1,0:T(8,128)S(1)}, u32[]{:S(2)}, u32[]{:S(2)}) async-start(f32[32,8,128]{2,1,0:T(8,128)} %get-tuple-element.26), calls=%async_computation | async-start | bytes 262144 | tf_op jit(solution)/shard_map/all_to_all | solution.py:302
  19.9 27.5 %collective-permute-start.4 = (bf16[2,304,128]{2,1,0:T(8,128)(2,1)S(1)}, bf16[2,304,128]{2,1,0:T(8,128)(2,1)S(1)}, u32[]{:S(2)}, u32[]{:S(2)}) collective-permute-start(bf16[2,304,128]{2,1,0:T(8,128)(2,1)S(1)} %pad_maximum_fusion.1), channel_id=1, source_target_pairs={{0,8},{1,7},{2,10},{3,9},{4,12},{5,11},{6,14},{7,13},{8,0},{9,15},... | collective-permute-start | bytes 466952 | tf_op jit(solution)/shard_map/ppermute | solution.py:304
  25.1 22.3 %collective-permute-start.3 = (bf16[2,304,128]{2,1,0:T(8,128)(2,1)S(1)}, bf16[2,304,128]{2,1,0:T(8,128)(2,1)S(1)}, u32[]{:S(2)}, u32[]{:S(2)}) collective-permute-start(bf16[2,304,128]{2,1,0:T(8,128)(2,1)S(1)} %pad_maximum_fusion.1), channel_id=1, source_target_pairs={{0,2},{1,11},{2,4},{3,13},{4,6},{5,15},{6,8},{7,1},{8,10},{9,3},{1... | collective-permute-start | bytes 466952 | tf_op jit(solution)/shard_map/ppermute | solution.py:304
  28.5 19.0 %collective-permute-start.2 = (bf16[2,304,128]{2,1,0:T(8,128)(2,1)S(1)}, bf16[2,304,128]{2,1,0:T(8,128)(2,1)S(1)}, u32[]{:S(2)}, u32[]{:S(2)}) collective-permute-start(bf16[2,304,128]{2,1,0:T(8,128)(2,1)S(1)} %pad_maximum_fusion.1), channel_id=1, source_target_pairs={{0,14},{1,5},{2,0},{3,7},{4,2},{5,9},{6,4},{7,11},{8,6},{9,13},{10... | collective-permute-start | bytes 466952 | tf_op jit(solution)/shard_map/ppermute | solution.py:304
  32.4 15.1 %collective-permute-start.1 = (bf16[2,304,128]{2,1,0:T(8,128)(2,1)S(1)}, bf16[2,304,128]{2,1,0:T(8,128)(2,1)S(1)}, u32[]{:S(2)}, u32[]{:S(2)}) collective-permute-start(bf16[2,304,128]{2,1,0:T(8,128)(2,1)S(1)} %pad_maximum_fusion.1), channel_id=1, source_target_pairs={{0,0},{1,13},{2,2},{3,15},{4,4},{5,1},{6,6},{7,3},{8,8},{9,5},{10,... | collective-permute-start | bytes 466952 | tf_op jit(solution)/shard_map/ppermute | solution.py:304
  36.0 0.9 copy-start
  36.9 12.9 %copy-start.8 = (s32[2,4]{1,0:T(2,128)S(1)}, s32[2,4]{1,0:T(2,128)}, u32[]{:S(2)}) copy-start(s32[2,4]{1,0:T(2,128)} %constant.65.clone) | copy-start | bytes 100
  38.2 23.8 %all-to-all-start.1 = ((bf16[32,16,304]{2,1,0:T(8,128)(2,1)}), bf16[32,16,304]{2,1,0:T(8,128)(2,1)S(1)}, u32[]{:S(2)}, u32[]{:S(2)}) async-start(bf16[32,16,304]{2,1,0:T(8,128)(2,1)} %shard_map.106), calls=%async_computation.1 | async-start | bytes 786432 | tf_op jit(solution)/shard_map/all_to_all | solution.py:308
  47.4 14.5 %copy-start.4 = (bf16[2,304,128]{2,1,0:T(8,128)(2,1)}, bf16[2,304,128]{2,1,0:T(8,128)(2,1)S(1)}, u32[]{:S(2)}) copy-start(bf16[2,304,128]{2,1,0:T(8,128)(2,1)S(1)} %collective-permute-done.4.q3_hbm) | copy-start | bytes 466948
  47.4 14.5 %copy-start.5 = (bf16[2,304,128]{2,1,0:T(8,128)(2,1)}, bf16[2,304,128]{2,1,0:T(8,128)(2,1)S(1)}, u32[]{:S(2)}) copy-start(bf16[2,304,128]{2,1,0:T(8,128)(2,1)S(1)} %collective-permute-done.3.q2_hbm) | copy-start | bytes 466948
  47.5 14.5 %copy-start.6 = (bf16[2,304,128]{2,1,0:T(8,128)(2,1)}, bf16[2,304,128]{2,1,0:T(8,128)(2,1)S(1)}, u32[]{:S(2)}) copy-start(bf16[2,304,128]{2,1,0:T(8,128)(2,1)S(1)} %collective-permute-done.2.q1_hbm) | copy-start | bytes 466948
  47.5 14.5 %copy-start.7 = (bf16[2,304,128]{2,1,0:T(8,128)(2,1)}, bf16[2,304,128]{2,1,0:T(8,128)(2,1)S(1)}, u32[]{:S(2)}) copy-start(bf16[2,304,128]{2,1,0:T(8,128)(2,1)S(1)} %collective-permute-done.1.q0_hbm) | copy-start | bytes 466948
  47.6 14.4 %collective-permute-start.5 = (bf16[8,304,128]{2,1,0:T(8,128)(2,1)S(1)}, bf16[8,304,128]{2,1,0:T(8,128)(2,1)S(1)}, u32[]{:S(2)}, u32[]{:S(2)}) collective-permute-start(bf16[8,304,128]{2,1,0:T(8,128)(2,1)S(1)} %pad_maximum_fusion), channel_id=1, source_target_pairs={{0,1},{1,0},{2,3},{3,2},{4,5},{5,4},{6,7},{7,6},{8,9},{9,8},{10,11... | collective-permute-start | bytes 1867784 | tf_op jit(solution)/shard_map/ppermute | solution.py:307
  61.9 0.7 copy-start.2
  62.0 0.9 copy-start.3
  72.9 7.7 %collective-permute-start.6 = (f32[8,304,128]{2,1,0:T(8,128)}, f32[8,304,128]{2,1,0:T(8,128)S(1)}, u32[]{:S(2)}, u32[]{:S(2)}) collective-permute-start(f32[8,304,128]{2,1,0:T(8,128)} %get-tuple-element.39), channel_id=1, source_target_pairs={{0,1},{1,0},{2,3},{3,2},{4,5},{5,4},{6,7},{7,6},{8,9},{9,8},{10,11... | collective-permute-start | bytes 3735560 | tf_op jit(solution)/shard_map/ppermute | solution.py:371
  76.5 19.0 %all-to-all-start.2 = ((bf16[32,16,304]{2,1,0:T(8,128)(2,1)}), bf16[32,16,304]{2,1,0:T(8,128)(2,1)S(1)}, u32[]{:S(2)}, u32[]{:S(2)}) async-start(bf16[32,16,304]{2,1,0:T(8,128)(2,1)} %get-tuple-element.41), calls=%async_computation.2 | async-start | bytes 786432 | tf_op jit(solution)/shard_map/all_to_all | solution.py:372
  82.0 13.5 %copy-start.1 = (f32[304,256]{1,0:T(8,128)S(1)}, f32[304,256]{1,0:T(8,128)}, u32[]{:S(2)}) copy-start(f32[304,256]{1,0:T(8,128)} %get-tuple-element.40.prim_ref) | copy-start | bytes 933892
  82.0 14.7 %collective-permute-start.10 = (bf16[2,304,128]{2,1,0:T(8,128)(2,1)S(1)}, bf16[2,304,128]{2,1,0:T(8,128)(2,1)S(1)}, u32[]{:S(2)}, u32[]{:S(2)}) collective-permute-start(bf16[2,304,128]{2,1,0:T(8,128)(2,1)S(1)} %get-tuple-element.46), channel_id=1, source_target_pairs={{0,8},{1,11},{2,10},{3,13},{4,12},{5,15},{6,14},{7,1},{8,0},{9,3},... | collective-permute-start | bytes 466952 | tf_op jit(solution)/shard_map/ppermute | solution.py:374
  84.5 14.2 %collective-permute-start.9 = (bf16[2,304,128]{2,1,0:T(8,128)(2,1)S(1)}, bf16[2,304,128]{2,1,0:T(8,128)(2,1)S(1)}, u32[]{:S(2)}, u32[]{:S(2)}) collective-permute-start(bf16[2,304,128]{2,1,0:T(8,128)(2,1)S(1)} %get-tuple-element.47), channel_id=1, source_target_pairs={{0,14},{1,7},{2,0},{3,9},{4,2},{5,11},{6,4},{7,13},{8,6},{9,15},{1... | collective-permute-start | bytes 466952 | tf_op jit(solution)/shard_map/ppermute | solution.py:374
  89.3 10.9 %collective-permute-start.8 = (bf16[2,304,128]{2,1,0:T(8,128)(2,1)S(1)}, bf16[2,304,128]{2,1,0:T(8,128)(2,1)S(1)}, u32[]{:S(2)}, u32[]{:S(2)}) collective-permute-start(bf16[2,304,128]{2,1,0:T(8,128)(2,1)S(1)} %get-tuple-element.48), channel_id=1, source_target_pairs={{0,2},{1,13},{2,4},{3,15},{4,6},{5,1},{6,8},{7,3},{8,10},{9,5},{10... | collective-permute-start | bytes 466952 | tf_op jit(solution)/shard_map/ppermute | solution.py:374
  91.2 10.1 %collective-permute-start.7 = (bf16[2,304,128]{2,1,0:T(8,128)(2,1)S(1)}, bf16[2,304,128]{2,1,0:T(8,128)(2,1)S(1)}, u32[]{:S(2)}, u32[]{:S(2)}) collective-permute-start(bf16[2,304,128]{2,1,0:T(8,128)(2,1)S(1)} %get-tuple-element.49), channel_id=1, source_target_pairs={{0,0},{1,5},{2,2},{3,7},{4,4},{5,9},{6,6},{7,11},{8,8},{9,13},{10,... | collective-permute-start | bytes 466952 | tf_op jit(solution)/shard_map/ppermute | solution.py:374
  101.5 3.3 %collective-permute-start.11 = (f32[304,128]{1,0:T(8,128)S(1)}, f32[304,128]{1,0:T(8,128)S(1)}, u32[]{:S(2)}, u32[]{:S(2)}) collective-permute-start(f32[304,128]{1,0:T(8,128)S(1)} %get-tuple-element.51), channel_id=1, source_target_pairs={{0,1},{1,0},{2,3},{3,2},{4,5},{5,4},{6,7},{7,6},{8,9},{9,8},{10,11... | collective-permute-start | bytes 466952 | tf_op jit(solution)/shard_map/ppermute | solution.py:378

commit v4 on v3

--- a/solution.py
+++ b/solution.py
@@ -166,7 +166,7 @@
 
 
 def grad_kernel(
-    columns_ref, count_ref, arrived_hbm, q0_hbm, q1_hbm, q2_hbm, q3_hbm, sib_hbm,
+    columns_ref, count_ref, arrived_hbm, q0_hbm, q1_hbm, q2_hbm, q3_hbm, sib0_hbm, sib1_hbm,
     comp_hbm, comp_t_hbm, slots_hbm, wrow_hbm, wt_hbm, label_hbm, value_hbm, weight_hbm,
     part_sib_hbm, part_own_hbm, prim_hbm, back_ref,
     arrived_ref, q_ref, comp_ref, comp_t_ref, slots_ref, w_scr, wt_scr, label_ref, value_ref, weight_ref,
@@ -175,14 +175,15 @@
     prim = wt_hbm.shape[1]
     slots = slots_ref.shape[0]
     dim = wt_hbm.shape[0]
-    half = sib_hbm.shape[0]
+    half = 2 * sib0_hbm.shape[0]
     copies = fetch(
         in_sems,
         (arrived_hbm, arrived_ref),
         (comp_hbm, comp_ref),
         (wrow_hbm, w_scr.at[:prim, :]),
         (wt_hbm, wt_scr.at[:, :prim]),
-        (sib_hbm, q_ref.at[:half]),
+        (sib0_hbm, q_ref.at[:half // 2]),
+        (sib1_hbm, q_ref.at[half // 2:half]),
         (slots_hbm, slots_ref),
         (label_hbm, label_ref),
         (value_hbm, value_ref),
@@ -301,12 +302,6 @@
     )(owner, row, query_feats.T, primary_w.T)
     wanted = lax.all_to_all(ask, "section", split_axis=0, concat_axis=0, tiled=True)
     both = jnp.stack([qp, lax.ppermute(qp, "leaf", sibling)])
-    own = [lax.ppermute(both, "leaf", hops(chips, k, 1)) for k in range(4)]
-    served = call(serve_kernel, shape((sections, CAP, dim), BF16), [VMEM] * 2)(wanted, wp)
-    own = after(own, served)
-    sib = lax.ppermute(jnp.concatenate(own), "leaf", sibling)
-    arrived = lax.all_to_all(served, "section", split_axis=0, concat_axis=0, tiled=True)
-
     first = (section_id * leaves + leaf_id) * prim
     numbers = jnp.stack([first, leaf_id * prim, jnp.int32(leaves * prim)]).astype(I32)
     weight = query_weight.reshape(1, -1)
@@ -326,6 +321,13 @@
         outs=(VMEM,) * 6 + (SMEM,),
     )(numbers, inv_prop, owner, row, wp, positive_label.T, positive_bucket.T, weight)
 
+    (wanted,) = after((wanted,), count)
+    served = call(serve_kernel, shape((sections, CAP, dim), BF16), [VMEM] * 2)(wanted, wp)
+    own = [lax.ppermute(both, "leaf", hops(chips, k, 1)) for k in range(4)]
+    arrived = lax.all_to_all(served, "section", split_axis=0, concat_axis=0, tiled=True)
+    late = after((jnp.concatenate(own[:2]),), arrived)[0]
+    sibs = [lax.ppermute(late, "leaf", sibling), lax.ppermute(jnp.concatenate(own[2:]), "leaf", sibling)]
+
     core = leaf_id % 2
     chip = leaf_id // 2
     near = jnp.array(HOPS, I32)
@@ -344,7 +346,7 @@
             shape((dim, prim), F32),
             shape((sections, CAP, dim), BF16),
         ),
-        [SMEM] * 2 + [ANY] * 14,
+        [SMEM] * 2 + [ANY] * 15,
         scratch=(
             pltpu.VMEM(arrived.shape, BF16),
             pltpu.VMEM((leaves, dim, queries), BF16),
@@ -361,12 +363,12 @@
             pltpu.VMEM((slots, STEP * LANES), F32),
             pltpu.VMEM((slots, STEP * LANES), BF16),
             pltpu.VMEM((n, dim), F32),
-            pltpu.SemaphoreType.DMA((14,)),
+            pltpu.SemaphoreType.DMA((15,)),
             pltpu.SemaphoreType.DMA((leaves // STEP + 1,)),
         ),
         vmem=BIG,
         outs=(ANY, ANY, ANY, VMEM),
-    )(columns, count, arrived, *own, sib, comp, comp_t, slot_ids, wrow, wp, key, value, weight)
+    )(columns, count, arrived, *own, *sibs, comp, comp_t, slot_ids, wrow, wp, key, value, weight)
 
     swapped = lax.ppermute(part_sib, "leaf", sibling)
     returned = lax.all_to_all(back, "section", split_axis=0, concat_axis=0, tiled=True)

time: 106 us -> 113 us (1.066)
  starting transfers between devices: 66.9 us -> 76.7 us
  waiting for transfers between devices: 13.6 us -> 11.2 us
    all_to_all x1, waiting for transfers between devices: 7.73 us -> 0.01 us  [on_device(): lax.all_to_all(served, 'section', split_axis=0, concat_axis=0, tiled=True)]
    ppermute x1 -> x2, starting transfers between devices: 2.12 us -> 8.81 us  [the longest x1 6.89 us: on_device(): lax.ppermute(jnp.concatenate(own[2:]), 'leaf', sibling)]
    all_to_all x1, starting transfers between devices: 7.52 us -> 13.9 us  [on_device(): lax.all_to_all(ask, 'section', split_axis=0, concat_axis=0, tiled=True)]
    ppermute x1, starting transfers between devices: 8.79 us -> 2.86 us  [on_device(): both = jnp.stack([qp, lax.ppermute(qp, 'leaf', sibling)])]
    all_to_all x1, starting transfers between devices: 4.04 us -> 9.32 us  [on_device(): lax.all_to_all(back, 'section', split_axis=0, concat_axis=0, tiled=True)]
    all_to_all x1, waiting for transfers between devices: 0.01 us -> 3.03 us  [on_device(): lax.all_to_all(ask, 'section', split_axis=0, concat_axis=0, tiled=True)]
    all_to_all x1, starting transfers between devices: 9.21 us -> 6.47 us  [on_device(): lax.all_to_all(served, 'section', split_axis=0, concat_axis=0, tiled=True)]
    ppermute x4, starting transfers between devices: 13.4 us -> 15.3 us  [on_device(): lax.ppermute(sums[2 * k:2 * k + 2], 'leaf', hops(chips, k, -1))]
  transfers between devices with their start and end apart: 15 -> 16, of which waited for: 5 -> 6; matrix products, arithmetic and copies ran while one was open for 4% -> 3% of each run, Pallas kernels for 5% -> 5%
where the time goes in v4:
time: 113 us; the launch traced here: 112 us
  starting transfers between devices  76.7 us (68%)
  Pallas kernels  17.3 us (15%)
  waiting for transfers between devices  11.2 us (10%)
  other arithmetic  3.67 us (3%)
  local copies, waits for them, and re-layouts  1.96 us (2%)
    ppermute x4, starting transfers between devices, on_device(): own = [lax.ppermute(both, 'leaf', hops(chips, k, 1)) for k in range(4)]  16.1 us
    ppermute x4, starting transfers between devices, on_device(): lax.ppermute(sums[2 * k:2 * k + 2], 'leaf', hops(chips, k, -1))  15.3 us
    all_to_all x1, starting transfers between devices, on_device(): lax.all_to_all(ask, 'section', split_axis=0, concat_axis=0, tiled=True)  13.9 us
    pallas_call x1, Pallas kernels, on_device(): call(grad_kernel, (shape((chips, dim, queries), F32), shape((chips, dim,...  10.1 us
    all_to_all x1, starting transfers between devices, on_device(): lax.all_to_all(back, 'section', split_axis=0, concat_axis=0, tiled=True)  9.32 us
    ppermute x1, starting transfers between devices, on_device(): lax.ppermute(jnp.concatenate(own[2:]), 'leaf', sibling)  6.89 us
    all_to_all x1, starting transfers between devices, on_device(): lax.all_to_all(served, 'section', split_axis=0, concat_axis=0, tiled=True)  6.47 us
    ppermute x4, waiting for transfers between devices, on_device(): lax.ppermute(sums[2 * k:2 * k + 2], 'leaf', hops(chips, k, -1))  6.07 us
  transfers between devices with their start and end apart: 16, of which 6 were waited for; matrix products, arithmetic and copies ran while one was open for 3% of the time, Pallas kernels for 5%

profile of v4, /device:TPU:1, one launch (start us, length us, event | category | flops | bytes accessed | tf_op | source)
XLA Modules:
  0.0 111.9 jit_solution(3266495914344719556)
XLA Ops:
  0.6 2.0 %shard_map.104 = (f32[32,8,128]{2,1,0:T(8,128)}, bf16[304,128]{1,0:T(8,128)(2,1)}, bf16[304,256]{1,0:T(8,128)(2,1)}) custom-call(s32[1,256]{1,0:T(1,128)} %bitcast.33, s32[1,256]{1,0:T(1,128)} %bitcast.35, bf16[300,128]{1,0:T(8,128)(2,1)} %bitcast.26, bf16[300,256]{1,0:T(8,128)(2,1)} %bitcast.25), custom_call_target="tpu_custom_call" | custom-call | tf_op jit(solution)/shard_map/pallas_call | solution.py:290
  2.7 13.9 %all-to-all-start = ((f32[32,8,128]{2,1,0:T(8,128)}), f32[32,8,128]{2,1,0:T(8,128)S(1)}, u32[]{:S(2)}, u32[]{:S(2)}) async-start(f32[32,8,128]{2,1,0:T(8,128)} %get-tuple-element.24), calls=%async_computation | async-start | bytes 262144 | tf_op jit(solution)/shard_map/all_to_all | solution.py:303
  16.5 2.9 %collective-permute-start = (bf16[304,128]{1,0:T(8,128)(2,1)}, bf16[304,128]{1,0:T(8,128)(2,1)S(1)}, u32[]{:S(2)}, u32[]{:S(2)}) collective-permute-start(bf16[304,128]{1,0:T(8,128)(2,1)} %get-tuple-element.26), channel_id=1, source_target_pairs={{0,1},{1,0},{2,3},{3,2},{4,5},{5,4},{6,7},{7,6},{8,9},{9,8},{10,11... | collective-permute-start | bytes 233480 | tf_op jit(solution)/shard_map/ppermute | solution.py:304
  20.1 2.8 %shard_map.105 = (bf16[256,512]{1,0:T(8,128)(2,1)}, bf16[512,256]{1,0:T(8,128)(2,1)}, s32[512,128]{1,0:T(8,128)}, bf16[256,304]{1,0:T(8,128)(2,1)}, s32[8,2048]{...) custom-call(s32[3]{0:T(128)} %pad_add_fusion.2.first_ref, f32[16]{0:T(128)} %prop_ref.1, s32[1,256]{1,0:T(1,128)} %bitcast.34, ...), custom_call_target="tpu_custom_call" | custom-call | tf_op jit(solution)/shard_map/pallas_call | solution.py:308
  22.8 3.0 %all-to-all-done.ask_ref = f32[32,8,128]{2,1,0:T(8,128)S(1)} async-done(((f32[32,8,128]{2,1,0:T(8,128)}), f32[32,8,128]{2,1,0:T(8,128)S(1)}, u32[]{:S(2)}, u32[]{:S(2)}) %all-to-all-start) | async-done | bytes 131104 | tf_op jit(solution)/shard_map/all_to_all | solution.py:303
  28.0 6.5 %all-to-all-start.1 = ((bf16[32,16,304]{2,1,0:T(8,128)(2,1)}), bf16[32,16,304]{2,1,0:T(8,128)(2,1)S(1)}, u32[]{:S(2)}, u32[]{:S(2)}) async-start(bf16[32,16,304]{2,1,0:T(8,128)(2,1)} %shard_map.106), calls=%async_computation.1 | async-start | bytes 786432 | tf_op jit(solution)/shard_map/all_to_all | solution.py:327
  34.6 5.2 %collective-permute-start.4 = (bf16[2,304,128]{2,1,0:T(8,128)(2,1)S(1)}, bf16[2,304,128]{2,1,0:T(8,128)(2,1)S(1)}, u32[]{:S(2)}, u32[]{:S(2)}) collective-permute-start(bf16[2,304,128]{2,1,0:T(8,128)(2,1)S(1)} %pad_maximum_fusion.2), channel_id=1, source_target_pairs={{0,8},{1,7},{2,10},{3,9},{4,12},{5,11},{6,14},{7,13},{8,0},{9,15},... | collective-permute-start | bytes 466952 | tf_op jit(solution)/shard_map/ppermute | solution.py:326
  39.8 3.4 %collective-permute-start.3 = (bf16[2,304,128]{2,1,0:T(8,128)(2,1)S(1)}, bf16[2,304,128]{2,1,0:T(8,128)(2,1)S(1)}, u32[]{:S(2)}, u32[]{:S(2)}) collective-permute-start(bf16[2,304,128]{2,1,0:T(8,128)(2,1)S(1)} %pad_maximum_fusion.2), channel_id=1, source_target_pairs={{0,2},{1,11},{2,4},{3,13},{4,6},{5,15},{6,8},{7,1},{8,10},{9,3},{1... | collective-permute-start | bytes 466952 | tf_op jit(solution)/shard_map/ppermute | solution.py:326
  43.2 3.9 %collective-permute-start.2 = (bf16[2,304,128]{2,1,0:T(8,128)(2,1)S(1)}, bf16[2,304,128]{2,1,0:T(8,128)(2,1)S(1)}, u32[]{:S(2)}, u32[]{:S(2)}) collective-permute-start(bf16[2,304,128]{2,1,0:T(8,128)(2,1)S(1)} %pad_maximum_fusion.2), channel_id=1, source_target_pairs={{0,14},{1,5},{2,0},{3,7},{4,2},{5,9},{6,4},{7,11},{8,6},{9,13},{10... | collective-permute-start | bytes 466952 | tf_op jit(solution)/shard_map/ppermute | solution.py:326
  47.2 3.6 %collective-permute-start.1 = (bf16[2,304,128]{2,1,0:T(8,128)(2,1)S(1)}, bf16[2,304,128]{2,1,0:T(8,128)(2,1)S(1)}, u32[]{:S(2)}, u32[]{:S(2)}) collective-permute-start(bf16[2,304,128]{2,1,0:T(8,128)(2,1)S(1)} %pad_maximum_fusion.2), channel_id=1, source_target_pairs={{0,0},{1,13},{2,2},{3,15},{4,4},{5,1},{6,6},{7,3},{8,8},{9,5},{10,... | collective-permute-start | bytes 466952 | tf_op jit(solution)/shard_map/ppermute | solution.py:326
  51.0 6.9 %collective-permute-start.6 = (bf16[4,304,128]{2,1,0:T(8,128)(2,1)S(1)}, bf16[4,304,128]{2,1,0:T(8,128)(2,1)S(1)}, u32[]{:S(2)}, u32[]{:S(2)}) collective-permute-start(bf16[4,304,128]{2,1,0:T(8,128)(2,1)S(1)} %pad_maximum_fusion.1), channel_id=1, source_target_pairs={{0,1},{1,0},{2,3},{3,2},{4,5},{5,4},{6,7},{7,6},{8,9},{9,8},{10,11... | collective-permute-start | bytes 933896 | tf_op jit(solution)/shard_map/ppermute | solution.py:329
  58.0 1.9 %collective-permute-start.5 = (bf16[4,304,128]{2,1,0:T(8,128)(2,1)S(1)}, bf16[4,304,128]{2,1,0:T(8,128)(2,1)S(1)}, u32[]{:S(2)}, u32[]{:S(2)}) collective-permute-start(bf16[4,304,128]{2,1,0:T(8,128)(2,1)S(1)} %pad_maximum_fusion), channel_id=1, source_target_pairs={{0,1},{1,0},{2,3},{3,2},{4,5},{5,4},{6,7},{7,6},{8,9},{9,8},{10,11... | collective-permute-start | bytes 933896 | tf_op jit(solution)/shard_map/ppermute | solution.py:329
  62.2 10.1 %shard_map.107 = (f32[8,304,128]{2,1,0:T(8,128)}, f32[8,304,128]{2,1,0:T(8,128)}, f32[304,256]{1,0:T(8,128)}, bf16[32,16,304]{2,1,0:T(8,128)(2,1)}) custom-call(s32[16]{0:T(128)} %pad_add_fusion.1.columns_ref, s32[16]{0:T(128)} %get-tuple-element.23.count_ref, bf16[32,16,304]{2,1,0:T(8,128)(2,1)} %copy-done.2, bf16[2,304,128]{2,1,0:T(8,128)(2,1)} %copy-done.6, ...), custom_call_target="tpu_custom_call" | custom-call | tf_op jit(solution)/shard_map/pallas_call | solution.py:341
  72.3 2.0 %collective-permute-start.7 = (f32[8,304,128]{2,1,0:T(8,128)}, f32[8,304,128]{2,1,0:T(8,128)S(1)}, u32[]{:S(2)}, u32[]{:S(2)}) collective-permute-start(f32[8,304,128]{2,1,0:T(8,128)} %get-tuple-element.35), channel_id=1, source_target_pairs={{0,1},{1,0},{2,3},{3,2},{4,5},{5,4},{6,7},{7,6},{8,9},{9,8},{10,11... | collective-permute-start | bytes 3735560 | tf_op jit(solution)/shard_map/ppermute | solution.py:373
  74.3 9.3 %all-to-all-start.2 = ((bf16[32,16,304]{2,1,0:T(8,128)(2,1)}), bf16[32,16,304]{2,1,0:T(8,128)(2,1)S(1)}, u32[]{:S(2)}, u32[]{:S(2)}) async-start(bf16[32,16,304]{2,1,0:T(8,128)(2,1)} %get-tuple-element.37), calls=%async_computation.2 | async-start | bytes 786432 | tf_op jit(solution)/shard_map/all_to_all | solution.py:374
  83.6 1.4 %add_convert_fusion = bf16[8,304,128]{2,1,0:T(8,128)(2,1)S(1)} fusion(f32[8,304,128]{2,1,0:T(8,128)} %get-tuple-element.34, f32[8,304,128]{2,1,0:T(8,128)S(1)} %collective-permute-done.7), kind=kLoop, calls=%fused_computation | loop fusion | flops 622592 | bytes 3112960 | tf_op jit(solution)/shard_map/convert_element_type | solution.py:375
  85.1 3.5 %collective-permute-start.11 = (bf16[2,304,128]{2,1,0:T(8,128)(2,1)S(1)}, bf16[2,304,128]{2,1,0:T(8,128)(2,1)S(1)}, u32[]{:S(2)}, u32[]{:S(2)}) collective-permute-start(bf16[2,304,128]{2,1,0:T(8,128)(2,1)S(1)} %get-tuple-element.42), channel_id=1, source_target_pairs={{0,8},{1,11},{2,10},{3,13},{4,12},{5,15},{6,14},{7,1},{8,0},{9,3},... | collective-permute-start | bytes 466952 | tf_op jit(solution)/shard_map/ppermute | solution.py:376
  88.6 3.7 %collective-permute-start.10 = (bf16[2,304,128]{2,1,0:T(8,128)(2,1)S(1)}, bf16[2,304,128]{2,1,0:T(8,128)(2,1)S(1)}, u32[]{:S(2)}, u32[]{:S(2)}) collective-permute-start(bf16[2,304,128]{2,1,0:T(8,128)(2,1)S(1)} %get-tuple-element.43), channel_id=1, source_target_pairs={{0,14},{1,7},{2,0},{3,9},{4,2},{5,11},{6,4},{7,13},{8,6},{9,15},{1... | collective-permute-start | bytes 466952 | tf_op jit(solution)/shard_map/ppermute | solution.py:376
  92.4 6.2 %collective-permute-start.9 = (bf16[2,304,128]{2,1,0:T(8,128)(2,1)S(1)}, bf16[2,304,128]{2,1,0:T(8,128)(2,1)S(1)}, u32[]{:S(2)}, u32[]{:S(2)}) collective-permute-start(bf16[2,304,128]{2,1,0:T(8,128)(2,1)S(1)} %get-tuple-element.44), channel_id=1, source_target_pairs={{0,2},{1,13},{2,4},{3,15},{4,6},{5,1},{6,8},{7,3},{8,10},{9,5},{10... | collective-permute-start | bytes 466952 | tf_op jit(solution)/shard_map/ppermute | solution.py:376
  98.5 1.9 %collective-permute-start.8 = (bf16[2,304,128]{2,1,0:T(8,128)(2,1)S(1)}, bf16[2,304,128]{2,1,0:T(8,128)(2,1)S(1)}, u32[]{:S(2)}, u32[]{:S(2)}) collective-permute-start(bf16[2,304,128]{2,1,0:T(8,128)(2,1)S(1)} %get-tuple-element.45), channel_id=1, source_target_pairs={{0,0},{1,5},{2,2},{3,7},{4,4},{5,9},{6,6},{7,11},{8,8},{9,13},{10,... | collective-permute-start | bytes 466952 | tf_op jit(solution)/shard_map/ppermute | solution.py:376
  101.7 1.4 %collective-permute-done.10 = bf16[2,304,128]{2,1,0:T(8,128)(2,1)S(1)} collective-permute-done((bf16[2,304,128]{2,1,0:T(8,128)(2,1)S(1)}, bf16[2,304,128]{2,1,0:T(8,128)(2,1)S(1)}, u32[]{:S(2)}, u32[]{:S(2)}) %collective-permute-start.10) | collective-permute-done | bytes 155680 | tf_op jit(solution)/shard_map/ppermute | solution.py:376
  103.2 1.8 %collective-permute-done.9 = bf16[2,304,128]{2,1,0:T(8,128)(2,1)S(1)} collective-permute-done((bf16[2,304,128]{2,1,0:T(8,128)(2,1)S(1)}, bf16[2,304,128]{2,1,0:T(8,128)(2,1)S(1)}, u32[]{:S(2)}, u32[]{:S(2)}) %collective-permute-start.9) | collective-permute-done | bytes 155680 | tf_op jit(solution)/shard_map/ppermute | solution.py:376
  105.0 2.8 %collective-permute-done.8 = bf16[2,304,128]{2,1,0:T(8,128)(2,1)S(1)} collective-permute-done((bf16[2,304,128]{2,1,0:T(8,128)(2,1)S(1)}, bf16[2,304,128]{2,1,0:T(8,128)(2,1)S(1)}, u32[]{:S(2)}, u32[]{:S(2)}) %collective-permute-start.8) | collective-permute-done | bytes 155680 | tf_op jit(solution)/shard_map/ppermute | solution.py:376
  107.9 1.9 %collective-permute-start.12 = (f32[304,128]{1,0:T(8,128)S(1)}, f32[304,128]{1,0:T(8,128)S(1)}, u32[]{:S(2)}, u32[]{:S(2)}) collective-permute-start(f32[304,128]{1,0:T(8,128)S(1)} %get-tuple-element.47), channel_id=1, source_target_pairs={{0,1},{1,0},{2,3},{3,2},{4,5},{5,4},{6,7},{7,6},{8,9},{9,8},{10,11... | collective-permute-start | bytes 466952 | tf_op jit(solution)/shard_map/ppermute | solution.py:380
  (51 shorter events, 8.8 us)
Async XLA Ops:
  2.6 31.9 %copy-start.9 = (bf16[304,128]{1,0:T(8,128)(2,1)S(1)}, bf16[304,128]{1,0:T(8,128)(2,1)}, u32[]{:S(2)}) copy-start(bf16[304,128]{1,0:T(8,128)(2,1)} %get-tuple-element.26) | copy-start | bytes 233476
  2.6 40.5 %copy-start.10 = (s32[2,4]{1,0:T(2,128)S(1)}, s32[2,4]{1,0:T(2,128)}, u32[]{:S(2)}) copy-start(s32[2,4]{1,0:T(2,128)} %constant.65.clone) | copy-start | bytes 100
  2.7 23.2 %all-to-all-start = ((f32[32,8,128]{2,1,0:T(8,128)}), f32[32,8,128]{2,1,0:T(8,128)S(1)}, u32[]{:S(2)}, u32[]{:S(2)}) async-start(f32[32,8,128]{2,1,0:T(8,128)} %get-tuple-element.24), calls=%async_computation | async-start | bytes 262144 | tf_op jit(solution)/shard_map/all_to_all | solution.py:303
  16.5 18.0 %collective-permute-start = (bf16[304,128]{1,0:T(8,128)(2,1)}, bf16[304,128]{1,0:T(8,128)(2,1)S(1)}, u32[]{:S(2)}, u32[]{:S(2)}) collective-permute-start(bf16[304,128]{1,0:T(8,128)(2,1)} %get-tuple-element.26), channel_id=1, source_target_pairs={{0,1},{1,0},{2,3},{3,2},{4,5},{5,4},{6,7},{7,6},{8,9},{9,8},{10,11... | collective-permute-start | bytes 233480 | tf_op jit(solution)/shard_map/ppermute | solution.py:304
  28.0 29.9 %all-to-all-start.1 = ((bf16[32,16,304]{2,1,0:T(8,128)(2,1)}), bf16[32,16,304]{2,1,0:T(8,128)(2,1)S(1)}, u32[]{:S(2)}, u32[]{:S(2)}) async-start(bf16[32,16,304]{2,1,0:T(8,128)(2,1)} %shard_map.106), calls=%async_computation.1 | async-start | bytes 786432 | tf_op jit(solution)/shard_map/all_to_all | solution.py:327
  34.6 16.3 %collective-permute-start.4 = (bf16[2,304,128]{2,1,0:T(8,128)(2,1)S(1)}, bf16[2,304,128]{2,1,0:T(8,128)(2,1)S(1)}, u32[]{:S(2)}, u32[]{:S(2)}) collective-permute-start(bf16[2,304,128]{2,1,0:T(8,128)(2,1)S(1)} %pad_maximum_fusion.2), channel_id=1, source_target_pairs={{0,8},{1,7},{2,10},{3,9},{4,12},{5,11},{6,14},{7,13},{8,0},{9,15},... | collective-permute-start | bytes 466952 | tf_op jit(solution)/shard_map/ppermute | solution.py:326
  39.8 11.1 %collective-permute-start.3 = (bf16[2,304,128]{2,1,0:T(8,128)(2,1)S(1)}, bf16[2,304,128]{2,1,0:T(8,128)(2,1)S(1)}, u32[]{:S(2)}, u32[]{:S(2)}) collective-permute-start(bf16[2,304,128]{2,1,0:T(8,128)(2,1)S(1)} %pad_maximum_fusion.2), channel_id=1, source_target_pairs={{0,2},{1,11},{2,4},{3,13},{4,6},{5,15},{6,8},{7,1},{8,10},{9,3},{1... | collective-permute-start | bytes 466952 | tf_op jit(solution)/shard_map/ppermute | solution.py:326
  43.2 14.7 %collective-permute-start.2 = (bf16[2,304,128]{2,1,0:T(8,128)(2,1)S(1)}, bf16[2,304,128]{2,1,0:T(8,128)(2,1)S(1)}, u32[]{:S(2)}, u32[]{:S(2)}) collective-permute-start(bf16[2,304,128]{2,1,0:T(8,128)(2,1)S(1)} %pad_maximum_fusion.2), channel_id=1, source_target_pairs={{0,14},{1,5},{2,0},{3,7},{4,2},{5,9},{6,4},{7,11},{8,6},{9,13},{10... | collective-permute-start | bytes 466952 | tf_op jit(solution)/shard_map/ppermute | solution.py:326
  47.2 10.7 %collective-permute-start.1 = (bf16[2,304,128]{2,1,0:T(8,128)(2,1)S(1)}, bf16[2,304,128]{2,1,0:T(8,128)(2,1)S(1)}, u32[]{:S(2)}, u32[]{:S(2)}) collective-permute-start(bf16[2,304,128]{2,1,0:T(8,128)(2,1)S(1)} %pad_maximum_fusion.2), channel_id=1, source_target_pairs={{0,0},{1,13},{2,2},{3,15},{4,4},{5,1},{6,6},{7,3},{8,8},{9,5},{10,... | collective-permute-start | bytes 466952 | tf_op jit(solution)/shard_map/ppermute | solution.py:326
  50.9 10.6 %copy-start.3 = (bf16[2,304,128]{2,1,0:T(8,128)(2,1)}, bf16[2,304,128]{2,1,0:T(8,128)(2,1)S(1)}, u32[]{:S(2)}) copy-start(bf16[2,304,128]{2,1,0:T(8,128)(2,1)S(1)} %collective-permute-done.4.q3_hbm) | copy-start | bytes 466948
  50.9 10.6 %copy-start.4 = (bf16[2,304,128]{2,1,0:T(8,128)(2,1)}, bf16[2,304,128]{2,1,0:T(8,128)(2,1)S(1)}, u32[]{:S(2)}) copy-start(bf16[2,304,128]{2,1,0:T(8,128)(2,1)S(1)} %collective-permute-done.3.q2_hbm) | copy-start | bytes 466948
  51.0 9.8 %collective-permute-start.6 = (bf16[4,304,128]{2,1,0:T(8,128)(2,1)S(1)}, bf16[4,304,128]{2,1,0:T(8,128)(2,1)S(1)}, u32[]{:S(2)}, u32[]{:S(2)}) collective-permute-start(bf16[4,304,128]{2,1,0:T(8,128)(2,1)S(1)} %pad_maximum_fusion.1), channel_id=1, source_target_pairs={{0,1},{1,0},{2,3},{3,2},{4,5},{5,4},{6,7},{7,6},{8,9},{9,8},{10,11... | collective-permute-start | bytes 933896 | tf_op jit(solution)/shard_map/ppermute | solution.py:329
  57.9 3.6 %copy-start.5 = (bf16[2,304,128]{2,1,0:T(8,128)(2,1)}, bf16[2,304,128]{2,1,0:T(8,128)(2,1)S(1)}, u32[]{:S(2)}) copy-start(bf16[2,304,128]{2,1,0:T(8,128)(2,1)S(1)} %collective-permute-done.2.q1_hbm) | copy-start | bytes 466948
  57.9 3.6 %copy-start.6 = (bf16[2,304,128]{2,1,0:T(8,128)(2,1)}, bf16[2,304,128]{2,1,0:T(8,128)(2,1)S(1)}, u32[]{:S(2)}) copy-start(bf16[2,304,128]{2,1,0:T(8,128)(2,1)S(1)} %collective-permute-done.1.q0_hbm) | copy-start | bytes 466948
  58.0 3.5 %copy-start.2 = (bf16[32,16,304]{2,1,0:T(8,128)(2,1)}, bf16[32,16,304]{2,1,0:T(8,128)(2,1)S(1)}, u32[]{:S(2)}) copy-start(bf16[32,16,304]{2,1,0:T(8,128)(2,1)S(1)} %all-to-all-done.1.arrived_hbm) | copy-start | bytes 933892
  58.0 3.5 %collective-permute-start.5 = (bf16[4,304,128]{2,1,0:T(8,128)(2,1)S(1)}, bf16[4,304,128]{2,1,0:T(8,128)(2,1)S(1)}, u32[]{:S(2)}, u32[]{:S(2)}) collective-permute-start(bf16[4,304,128]{2,1,0:T(8,128)(2,1)S(1)} %pad_maximum_fusion), channel_id=1, source_target_pairs={{0,1},{1,0},{2,3},{3,2},{4,5},{5,4},{6,7},{7,6},{8,9},{9,8},{10,11... | collective-permute-start | bytes 933896 | tf_op jit(solution)/shard_map/ppermute | solution.py:329
  72.3 11.4 %collective-permute-start.7 = (f32[8,304,128]{2,1,0:T(8,128)}, f32[8,304,128]{2,1,0:T(8,128)S(1)}, u32[]{:S(2)}, u32[]{:S(2)}) collective-permute-start(f32[8,304,128]{2,1,0:T(8,128)} %get-tuple-element.35), channel_id=1, source_target_pairs={{0,1},{1,0},{2,3},{3,2},{4,5},{5,4},{6,7},{7,6},{8,9},{9,8},{10,11... | collective-permute-start | bytes 3735560 | tf_op jit(solution)/shard_map/ppermute | solution.py:373
  74.3 26.2 %all-to-all-start.2 = ((bf16[32,16,304]{2,1,0:T(8,128)(2,1)}), bf16[32,16,304]{2,1,0:T(8,128)(2,1)S(1)}, u32[]{:S(2)}, u32[]{:S(2)}) async-start(bf16[32,16,304]{2,1,0:T(8,128)(2,1)} %get-tuple-element.37), calls=%async_computation.2 | async-start | bytes 786432 | tf_op jit(solution)/shard_map/all_to_all | solution.py:374
  85.1 15.4 %copy-start.1 = (f32[304,256]{1,0:T(8,128)S(1)}, f32[304,256]{1,0:T(8,128)}, u32[]{:S(2)}) copy-start(f32[304,256]{1,0:T(8,128)} %get-tuple-element.36.prim_ref) | copy-start | bytes 933892
  85.1 16.6 %collective-permute-start.11 = (bf16[2,304,128]{2,1,0:T(8,128)(2,1)S(1)}, bf16[2,304,128]{2,1,0:T(8,128)(2,1)S(1)}, u32[]{:S(2)}, u32[]{:S(2)}) collective-permute-start(bf16[2,304,128]{2,1,0:T(8,128)(2,1)S(1)} %get-tuple-element.42), channel_id=1, source_target_pairs={{0,8},{1,11},{2,10},{3,13},{4,12},{5,15},{6,14},{7,1},{8,0},{9,3},... | collective-permute-start | bytes 466952 | tf_op jit(solution)/shard_map/ppermute | solution.py:376
  88.6 14.5 %collective-permute-start.10 = (bf16[2,304,128]{2,1,0:T(8,128)(2,1)S(1)}, bf16[2,304,128]{2,1,0:T(8,128)(2,1)S(1)}, u32[]{:S(2)}, u32[]{:S(2)}) collective-permute-start(bf16[2,304,128]{2,1,0:T(8,128)(2,1)S(1)} %get-tuple-element.43), channel_id=1, source_target_pairs={{0,14},{1,7},{2,0},{3,9},{4,2},{5,11},{6,4},{7,13},{8,6},{9,15},{1... | collective-permute-start | bytes 466952 | tf_op jit(solution)/shard_map/ppermute | solution.py:376
  92.4 12.6 %collective-permute-start.9 = (bf16[2,304,128]{2,1,0:T(8,128)(2,1)S(1)}, bf16[2,304,128]{2,1,0:T(8,128)(2,1)S(1)}, u32[]{:S(2)}, u32[]{:S(2)}) collective-permute-start(bf16[2,304,128]{2,1,0:T(8,128)(2,1)S(1)} %get-tuple-element.44), channel_id=1, source_target_pairs={{0,2},{1,13},{2,4},{3,15},{4,6},{5,1},{6,8},{7,3},{8,10},{9,5},{10... | collective-permute-start | bytes 466952 | tf_op jit(solution)/shard_map/ppermute | solution.py:376
  98.5 9.3 %collective-permute-start.8 = (bf16[2,304,128]{2,1,0:T(8,128)(2,1)S(1)}, bf16[2,304,128]{2,1,0:T(8,128)(2,1)S(1)}, u32[]{:S(2)}, u32[]{:S(2)}) collective-permute-start(bf16[2,304,128]{2,1,0:T(8,128)(2,1)S(1)} %get-tuple-element.45), channel_id=1, source_target_pairs={{0,0},{1,5},{2,2},{3,7},{4,4},{5,9},{6,6},{7,11},{8,8},{9,13},{10,... | collective-permute-start | bytes 466952 | tf_op jit(solution)/shard_map/ppermute | solution.py:376
  107.9 3.3 %collective-permute-start.12 = (f32[304,128]{1,0:T(8,128)S(1)}, f32[304,128]{1,0:T(8,128)S(1)}, u32[]{:S(2)}, u32[]{:S(2)}) collective-permute-start(f32[304,128]{1,0:T(8,128)S(1)} %get-tuple-element.47), channel_id=1, source_target_pairs={{0,1},{1,0},{2,3},{3,2},{4,5},{5,4},{6,7},{7,6},{8,9},{9,8},{10,11... | collective-permute-start | bytes 466952 | tf_op jit(solution)/shard_map/ppermute | solution.py:380
  (3 other events, 2.4 us)
